TPU v7x, 128 devices: a whole 4x4x4 slice. The times are simulated.
128 devices in a mesh: node: 8 (over z, core), local: 16 (over x, y).
Axes of the slice: x: 4, y: 4, z: 4, core: 2. Of those that a mesh axis runs over, the one named last changes fastest.
Arguments:
- latent: bfloat16 [16384, 1024], P(('node', 'local')), may hold values from -6 to 6
- grad_out: bfloat16 [16384, 1024], P(('node', 'local')), may hold values from -6 to 6
- expert_ids: int32 [16384, 4], P(('node', 'local')), may hold values from 0 to 127, all different within a row; in each aligned block of 128 rows (0 to 127, 128 to 255, ...) at most 6 rows name the same one
- combine: bfloat16 [16384, 4], P(('node', 'local')), may hold values from 0.099609375 to 0.59765625
- w_up: bfloat16 [128, 2, 1024, 1344], P(('node', 'local')), may hold values from -0.1875 to 0.1875
- w_down: bfloat16 [128, 2, 1344, 1024], P(('node', 'local')), may hold values from -0.125 to 0.125
Outputs:
- d_latent: bfloat16 [16384, 1024], P(('node', 'local'))
- d_combine: float32 [16384, 4], P(('node', 'local'))
- d_up: bfloat16 [128, 2, 1024, 1344], P(('node', 'local'))
- d_down: bfloat16 [128, 2, 1344, 1024], P(('node', 'local'))
Inputs may be any that keep to these rules, and one draw needn't show every extreme that they name: `expert_ids`: each row names 4 different experts. Within the rows of one device (aligned blocks of 128 rows) no expert is named by more than 6 rows, a bound that some block reaches.
All inputs are finite; a program needn't handle non-finite values.
Results may differ from a plain program's by a relative error of at most 0.005.
Values may be sent and summed in bfloat16 or wider, within the bound.
No kernel may reach another device: no remote copies, remote signals or barrier semaphores. Data moves between devices by JAX's collectives and lax.ppermute only.
A program may use at most 192 MiB of HBM per device.

v0:
```python
import jax
import jax.numpy as jnp
from jax import lax
from jax.sharding import PartitionSpec as P


def block_ranks(id_rows, count):
    onehot = (id_rows[..., None] == jnp.arange(count, dtype=jnp.int32)).astype(jnp.int32)
    before = jnp.cumsum(onehot, axis=-2) - onehot
    return jnp.sum(before * onehot, axis=-1)


def batched_backward(rows_in, rows_grad, rows_mix, upper, lower):
    pre = jnp.einsum("erl,elh->erh", rows_in, upper, preferred_element_type=jnp.float32)
    active = jnp.maximum(pre, 0.0)
    squared = active * active
    pulled = jnp.einsum("erl,ehl->erh", rows_grad, lower, preferred_element_type=jnp.float32)
    mixing = rows_mix.astype(jnp.float32)[..., None]
    mix_grad = jnp.sum(squared * pulled, axis=-1)
    hidden_grad = (2.0 * mixing * pulled * active).astype(jnp.bfloat16)
    input_grad = jnp.einsum("erh,elh->erl", hidden_grad, upper, preferred_element_type=jnp.float32)
    upper_grad = jnp.einsum(
        "erl,erh->elh", rows_in, hidden_grad, preferred_element_type=jnp.float32
    )
    scaled = (squared * mixing).astype(jnp.bfloat16)
    lower_grad = jnp.einsum("erh,erl->ehl", scaled, rows_grad, preferred_element_type=jnp.float32)
    return (input_grad, mix_grad, upper_grad.astype(jnp.bfloat16), lower_grad.astype(jnp.bfloat16))


def fill_rows(table, rows_in, rows_grad, mix_rows):
    pick_width = mix_rows.shape[1]
    valid = table >= 0
    safe = jnp.where(valid, table, 0)
    token_rows = safe // pick_width
    sent_in = jnp.where(valid[:, None], rows_in[token_rows], jnp.zeros((), rows_in.dtype))
    sent_grad = jnp.where(valid[:, None], rows_grad[token_rows], jnp.zeros((), rows_grad.dtype))
    sent_mix = jnp.where(valid, mix_rows.reshape(-1)[safe], jnp.zeros((), mix_rows.dtype))
    return (sent_in, sent_grad, sent_mix)


def on_device(latent, grad_out, expert_ids, combine, w_up, w_down):
    node_count = lax.axis_size("node")
    local_count = lax.axis_size("local")
    owner_count = node_count * local_count
    token_count, latent_width = latent.shape
    pick_width = expert_ids.shape[1]
    exp_local = w_up.shape[1]
    expert_count = owner_count // 2 * exp_local
    cap_slots = max(2, 3 * token_count * pick_width // (2 * expert_count))
    upper = w_up[0]
    lower = w_down[0]
    flat_ids = expert_ids.reshape(-1)
    ranks = block_ranks(flat_ids, expert_count)
    groups = flat_ids // exp_local
    inner = flat_ids % exp_local
    first_slot = (inner * owner_count + 2 * groups) * cap_slots + ranks
    second_slot = first_slot + cap_slots
    half_slot = (inner * (owner_count // 2) + groups) * cap_slots + ranks
    picks = jnp.arange(token_count * pick_width, dtype=jnp.int32)
    total_slots = exp_local * owner_count * cap_slots
    table = (
        jnp.full((total_slots,), -1, jnp.int32).at[first_slot].set(picks).at[second_slot].set(picks)
    )
    sent_in, sent_grad, sent_mix = fill_rows(table, latent, grad_out, combine)
    slot_shape = (exp_local, owner_count, cap_slots)
    recv_in, recv_grad, recv_mix = (
        lax.all_to_all(
            sent_in.reshape(slot_shape + (latent_width,)),
            ("node", "local"),
            split_axis=1,
            concat_axis=1,
            tiled=True,
        ),
        lax.all_to_all(
            sent_grad.reshape(slot_shape + (latent_width,)),
            ("node", "local"),
            split_axis=1,
            concat_axis=1,
            tiled=True,
        ),
        lax.all_to_all(
            sent_mix.reshape(slot_shape), ("node", "local"), split_axis=1, concat_axis=1, tiled=True
        ),
    )
    flat_shape = (exp_local, owner_count * cap_slots)
    part_in, part_mix, d_up, d_down = batched_backward(
        recv_in.reshape(flat_shape + (latent_width,)),
        recv_grad.reshape(flat_shape + (latent_width,)),
        recv_mix.reshape(flat_shape),
        upper,
        lower,
    )
    back_in, back_mix = (
        lax.all_to_all(
            part_in.reshape(slot_shape + (latent_width,)),
            ("node", "local"),
            split_axis=1,
            concat_axis=1,
            tiled=True,
        ),
        lax.all_to_all(
            part_mix.reshape(slot_shape), ("node", "local"), split_axis=1, concat_axis=1, tiled=True
        ),
    )
    rows_back = (
        back_in.reshape(exp_local, owner_count // 2, 2, cap_slots, latent_width)
        .sum(axis=2)
        .reshape(-1, latent_width)
    )
    lat_grad = rows_back[half_slot].reshape(token_count, pick_width, latent_width).sum(axis=1)
    mix_back = back_mix.reshape(exp_local, owner_count // 2, 2, cap_slots).sum(axis=2).reshape(-1)
    mix_grad = mix_back[half_slot].reshape(token_count, pick_width)
    return (lat_grad.astype(jnp.bfloat16), mix_grad, d_up[None], d_down[None])


def solution(mesh):
    in_specs = (
        P(("node", "local"), None),
        P(("node", "local"), None),
        P(("node", "local"), None),
        P(("node", "local"), None),
        P(("node", "local"), None, None, None),
        P(("node", "local"), None, None, None),
    )
    out_specs = (
        P(("node", "local"), None),
        P(("node", "local"), None),
        P(("node", "local"), None, None, None),
        P(("node", "local"), None, None, None),
    )
    return jax.shard_map(
        on_device, mesh=mesh, in_specs=in_specs, out_specs=out_specs, check_vma=False
    )
```

profile of v0, /device:TPU:1, one launch (start us, length us, event | category | flops | bytes accessed | tf_op | source)
XLA Modules:
  0.0 298.5 jit_solution(8207415050575964412)
XLA Ops:
  0.6 0.8 copy.61
  1.6 0.1 eq.27
  1.7 0.1 reshape.287
  1.8 0.8 copy.66
  2.6 0.1 reshape.289
  2.7 0.1 copy.64
  2.9 0.2 fusion.14
  3.2 0.2 fusion.13
  3.5 2.5 scatter_custom_fusion
  5.9 2.5 scatter_fusion
  8.4 9.5 %gather_fusion = bf16[1536]{0:T(1024)(128)(2,1)S(1)} fusion(bf16[512]{0:T(512)(128)(2,1)S(1)} %reshape.289, s32[2048]{0:T(1024)S(1)} %pad_clamp_fusion.1), kind=kCustom, calls=%fused_computation | custom fusion | bytes 12288 | tf_op jit(solution)/shard_map/gather | solution.py:37
  17.9 0.2 reshape.290
  18.1 0.7 copy.67
  18.8 11.8 %all-to-all-start = ((bf16[2,128,6]{2,0,1:T(2,128)(2,1)}), bf16[2,128,6]{2,0,1:T(2,128)(2,1)S(1)}, u32[]{:S(2)}, u32[]{:S(2)}) async-start(bf16[2,128,6]{2,0,1:T(2,128)(2,1)} %copy.67), calls=%async_computation | async-start | bytes 131072 | tf_op jit(solution)/shard_map/all_to_all | solution.py:81
  30.6 0.2 broadcast_in_dim.51
  30.8 5.1 %gather_fusion.2 = bf16[1536,1024]{1,0:T(8,128)(2,1)S(1)} fusion(bf16[128,1024]{1,0:T(8,128)(2,1)S(1)} %copy-done, s32[2048]{0:T(1024)S(1)} %pad_clamp_fusion), kind=kCustom, calls=%fused_computation.2 | custom fusion | bytes 6297600 | tf_op jit(solution)/shard_map/gather | solution.py:35
  35.9 2.8 gather.23
  38.7 5.1 %gather_fusion.1 = bf16[1536,1024]{1,0:T(8,128)(2,1)S(1)} fusion(bf16[128,1024]{1,0:T(8,128)(2,1)S(1)} %copy-done.2, s32[2048]{0:T(1024)S(1)} %pad_clamp_fusion), kind=kCustom, calls=%fused_computation.1 | custom fusion | bytes 6297600 | tf_op jit(solution)/shard_map/gather | solution.py:36
  43.8 2.8 gather.21
  46.6 5.2 %broadcast_select_fusion = (bf16[2,128,6,1024]{3,2,1,0:T(8,128)(2,1)S(1)}, bf16[2,128,6,1024]{3,2,1,0:T(8,128)(2,1)}) fusion(bf16[2,128,6,1024]{3,2,1,0:T(8,128)(2,1)} %gather.23, pred[2,128,6]{2,1,0:T(8,128)(4,1)S(1)} %broadcast_in_dim.51, bf16[2,128,6,1024]{3,2,1,0:T(8,128)(2,1)} %gather.21), kind=kLoop, calls=%fused_computation.19 | loop fusion | flops 3145728 | bytes 12584448 | tf_op jit(solution)/shard_map/jit(_where)/select_n | solution.py:35
  51.9 8.0 %copy.72 = bf16[2,128,6,1024]{3,0,2,1:T(2,128)(2,1)} copy(bf16[2,128,6,1024]{3,2,1,0:T(8,128)(2,1)S(1)} %get-tuple-element.29) | data formatting | bytes 6291456 | tf_op jit(solution)/shard_map/jit(_where)/select_n | solution.py:35
  59.8 10.1 %all-to-all-start.2 = ((bf16[2,128,6,1024]{3,0,2,1:T(2,128)(2,1)}), bf16[2,128,6,1024]{3,0,2,1:T(2,128)(2,1)S(1)}, u32[]{:S(2)}, u32[]{:S(2)}) async-start(bf16[2,128,6,1024]{3,0,2,1:T(2,128)(2,1)} %copy.72), calls=%async_computation.2 | async-start | bytes 6291456 | tf_op jit(solution)/shard_map/all_to_all | solution.py:67
  69.9 10.3 %copy.70 = bf16[2,128,6,1024]{3,0,2,1:T(2,128)(2,1)} copy(bf16[2,128,6,1024]{3,2,1,0:T(8,128)(2,1)} %get-tuple-element.30) | data formatting | bytes 6291456 | tf_op jit(solution)/shard_map/jit(_where)/select_n | solution.py:36
  80.2 30.6 %all-to-all-done.2 = bf16[2,128,6,1024]{3,0,2,1:T(2,128)(2,1)S(1)} async-done(((bf16[2,128,6,1024]{3,0,2,1:T(2,128)(2,1)}), bf16[2,128,6,1024]{3,0,2,1:T(2,128)(2,1)S(1)}, u32[]{:S(2)}, u32[]{:S(2)}) %all-to-all-start.2) | async-done | bytes 3145760 | tf_op jit(solution)/shard_map/all_to_all | solution.py:67
  110.9 5.4 %all-to-all-start.1 = ((bf16[2,128,6,1024]{3,0,2,1:T(2,128)(2,1)}), bf16[2,128,6,1024]{3,0,2,1:T(2,128)(2,1)}, u32[]{:S(2)}, u32[]{:S(2)}) async-start(bf16[2,128,6,1024]{3,0,2,1:T(2,128)(2,1)} %copy.70), calls=%async_computation.1 | async-start | bytes 6291456 | tf_op jit(solution)/shard_map/all_to_all | solution.py:74
  116.4 0.1 copy.69
  116.5 0.1 reshape.301
  116.7 9.2 %fusion.2 = f32[2,768,1344]{1,2,0:T(8,128)} fusion(bf16[1,2,1024,1344]{2,3,1,0:T(8,128)(2,1)} %param.10, bf16[2,768,1024]{2,0,1:T(2,128)(2,1)S(1)} %bitcast.43), kind=kOutput, calls=%fused_computation.13 | convolution fusion | flops 4227858432 | bytes 16908288 | tf_op jit(solution)/shard_map/erl,elh->erh/dot_general | solution.py:14
  125.9 31.1 %all-to-all-done.1 = bf16[2,128,6,1024]{3,0,2,1:T(2,128)(2,1)} async-done(((bf16[2,128,6,1024]{3,0,2,1:T(2,128)(2,1)}), bf16[2,128,6,1024]{3,0,2,1:T(2,128)(2,1)}, u32[]{:S(2)}, u32[]{:S(2)}) %all-to-all-start.1) | async-done | bytes 3145760 | tf_op jit(solution)/shard_map/all_to_all | solution.py:74
  157.0 13.2 %multiply_reduce_fusion = (f32[2,768]{1,0:T(2,128)S(1)}, bf16[2,768,1344]{1,2,0:T(8,128)(2,1)}) fusion(f32[2,768,1344]{1,2,0:T(8,128)} %fusion.2, f32[2,768]{1,0:T(2,128)S(1)} %broadcast_multiply_fusion, bf16[1,2,1344,1024]{3,2,1,0:T(8,128)(2,1)} %param.11, bf16[2,768,1024]{2,0,1:T(2,128)(2,1)} %bitcast.6), kind=kOutput, calls=%fused_computation.8 | convolution fusion | flops 4242307584 | bytes 21049344 | tf_op jit(solution)/shard_map/erl,ehl->erh/dot_general | solution.py:17
  170.3 0.1 reshape.297
  170.4 0.8 copy.76
  171.2 5.0 %all-to-all-start.4 = ((f32[2,128,6]{2,0,1:T(2,128)}), f32[2,128,6]{2,0,1:T(2,128)S(1)}, u32[]{:S(2)}, u32[]{:S(2)}) async-start(f32[2,128,6]{2,0,1:T(2,128)} %copy.76), calls=%async_computation.4 | async-start | bytes 262144 | tf_op jit(solution)/shard_map/all_to_all | solution.py:101
  176.2 8.4 %fusion = f32[2,768,1024]{2,1,0:T(8,128)S(1)} fusion(bf16[2,768,1344]{1,2,0:T(8,128)(2,1)} %get-tuple-element.28, bf16[1,2,1024,1344]{2,3,1,0:T(8,128)(2,1)} %param.10), kind=kOutput, calls=%fused_computation.11 | convolution fusion | flops 4227858432 | bytes 15925248 | tf_op jit(solution)/shard_map/erh,elh->erl/dot_general | solution.py:21
  184.6 7.4 %copy.74 = f32[2,768,1024]{2,0,1:T(2,128)} copy(f32[2,768,1024]{2,1,0:T(8,128)S(1)} %fusion) | data formatting | bytes 12582912 | tf_op jit(solution)/shard_map/erh,elh->erl/dot_general | solution.py:21
  192.0 10.5 %all-to-all-start.3 = ((f32[2,128,6,1024]{3,0,2,1:T(2,128)}), f32[2,128,6,1024]{3,0,2,1:T(2,128)}, u32[]{:S(2)}, u32[]{:S(2)}) async-start(f32[2,128,6,1024]{3,0,2,1:T(2,128)} %bitcast.42), calls=%async_computation.3 | async-start | bytes 12582912 | tf_op jit(solution)/shard_map/all_to_all | solution.py:94
  202.6 8.5 %convert_bitcast_fusion.1 = bf16[1,2,1024,1344]{2,3,1,0:T(8,128)(2,1)} fusion(bf16[2,768,1344]{1,2,0:T(8,128)(2,1)} %get-tuple-element.28, bf16[2,768,1024]{2,0,1:T(2,128)(2,1)S(1)} %bitcast.44), kind=kOutput, calls=%fused_computation.18 | convolution fusion | flops 4230610944 | bytes 12779520 | tf_op jit(solution)/shard_map/erl,erh->elh/dot_general | solution.py:22
  211.0 11.2 %convert_bitcast_fusion = bf16[1,2,1344,1024]{3,2,1,0:T(8,128)(2,1)} fusion(f32[2,768,1344]{1,2,0:T(8,128)} %fusion.2, f32[2,768]{1,0:T(2,128)S(1)} %reshape.301, bf16[2,768,1024]{2,0,1:T(2,128)(2,1)} %bitcast.6), kind=kOutput, calls=%fused_computation.17 | convolution fusion | flops 4238868480 | bytes 16914432 | tf_op jit(solution)/shard_map/erh,erl->ehl/dot_general | solution.py:26
  222.3 0.1 reshape.299
  222.5 2.5 gather_fusion.4
  225.1 0.7 copy.80
  225.7 52.2 %all-to-all-done.3 = f32[2,128,6,1024]{3,0,2,1:T(2,128)} async-done(((f32[2,128,6,1024]{3,0,2,1:T(2,128)}), f32[2,128,6,1024]{3,0,2,1:T(2,128)}, u32[]{:S(2)}, u32[]{:S(2)}) %all-to-all-start.3) | async-done | bytes 6291488 | tf_op jit(solution)/shard_map/all_to_all | solution.py:94
  278.0 7.5 %bitcast_reduce_fusion = f32[2,64,6,1024]{3,0,2,1:T(2,128)S(1)} fusion(f32[2,128,6,1024]{3,0,2,1:T(2,128)} %all-to-all-done.3), kind=kLoop, calls=%fused_computation.10 | loop fusion | flops 786432 | bytes 9437184 | tf_op jit(solution)/shard_map/reduce_sum | solution.py:107
  285.5 2.9 copy.75
  288.5 3.1 %reshape.295 = f32[768,1024]{1,0:T(8,128)S(1)} reshape(f32[2,64,6,1024]{3,2,1,0:T(8,128)} %copy.75) | data formatting | bytes 6291456 | tf_op jit(solution)/shard_map/reshape | solution.py:108
  291.5 2.7 gather_fusion.3
  294.2 1.9 reshape.296
  296.1 2.1 reduce_sum.50
  (35 shorter events, 0.6 us)
Async XLA Ops:
  0.6 30.2 %copy-start = (bf16[128,1024]{1,0:T(8,128)(2,1)S(1)}, bf16[128,1024]{1,0:T(8,128)(2,1)}, u32[]{:S(2)}) copy-start(bf16[128,1024]{1,0:T(8,128)(2,1)} %param.6) | copy-start | bytes 786436
  18.8 41.1 %all-to-all-start = ((bf16[2,128,6]{2,0,1:T(2,128)(2,1)}), bf16[2,128,6]{2,0,1:T(2,128)(2,1)S(1)}, u32[]{:S(2)}, u32[]{:S(2)}) async-start(bf16[2,128,6]{2,0,1:T(2,128)(2,1)} %copy.67), calls=%async_computation | async-start | bytes 131072 | tf_op jit(solution)/shard_map/all_to_all | solution.py:81
  35.9 2.8 copy-start.2
  59.8 51.0 %all-to-all-start.2 = ((bf16[2,128,6,1024]{3,0,2,1:T(2,128)(2,1)}), bf16[2,128,6,1024]{3,0,2,1:T(2,128)(2,1)S(1)}, u32[]{:S(2)}, u32[]{:S(2)}) async-start(bf16[2,128,6,1024]{3,0,2,1:T(2,128)(2,1)} %copy.72), calls=%async_computation.2 | async-start | bytes 6291456 | tf_op jit(solution)/shard_map/all_to_all | solution.py:67
  110.9 15.1 %copy-start.3 = (bf16[2,128,6,1024]{3,0,2,1:T(2,128)(2,1)}, bf16[2,128,6,1024]{3,0,2,1:T(2,128)(2,1)S(1)}, u32[]{:S(2)}) copy-start(bf16[2,128,6,1024]{3,0,2,1:T(2,128)(2,1)S(1)} %all-to-all-done.2) | copy-start | bytes 9437188
  110.9 46.2 %all-to-all-start.1 = ((bf16[2,128,6,1024]{3,0,2,1:T(2,128)(2,1)}), bf16[2,128,6,1024]{3,0,2,1:T(2,128)(2,1)}, u32[]{:S(2)}, u32[]{:S(2)}) async-start(bf16[2,128,6,1024]{3,0,2,1:T(2,128)(2,1)} %copy.70), calls=%async_computation.1 | async-start | bytes 6291456 | tf_op jit(solution)/shard_map/all_to_all | solution.py:74
  171.2 20.8 %all-to-all-start.4 = ((f32[2,128,6]{2,0,1:T(2,128)}), f32[2,128,6]{2,0,1:T(2,128)S(1)}, u32[]{:S(2)}, u32[]{:S(2)}) async-start(f32[2,128,6]{2,0,1:T(2,128)} %copy.76), calls=%async_computation.4 | async-start | bytes 262144 | tf_op jit(solution)/shard_map/all_to_all | solution.py:101
  192.0 10.5 %copy-start.4 = (bf16[2,128,6,1024]{3,0,2,1:T(2,128)(2,1)S(1)}, bf16[2,128,6,1024]{3,0,2,1:T(2,128)(2,1)}, u32[]{:S(2)}) copy-start(bf16[2,128,6,1024]{3,0,2,1:T(2,128)(2,1)} %copy-done.3) | copy-start | bytes 9437188
  192.0 86.0 %all-to-all-start.3 = ((f32[2,128,6,1024]{3,0,2,1:T(2,128)}), f32[2,128,6,1024]{3,0,2,1:T(2,128)}, u32[]{:S(2)}, u32[]{:S(2)}) async-start(f32[2,128,6,1024]{3,0,2,1:T(2,128)} %bitcast.42), calls=%async_computation.3 | async-start | bytes 12582912 | tf_op jit(solution)/shard_map/all_to_all | solution.py:94
  291.5 6.7 %copy-start.1 = (bf16[128,1024]{1,0:T(8,128)(2,1)S(1)}, bf16[128,1024]{1,0:T(8,128)(2,1)}, u32[]{:S(2)}) copy-start(bf16[128,1024]{1,0:T(8,128)(2,1)} %param.6) | copy-start | bytes 786436
where the time goes:
time: 303 us; the launch traced here: 298 us
  waiting for transfers between devices  114 us (38%)
  local copies, waits for them, and re-layouts  74.4 us (25%)
  matrix products  50.5 us (17%)
  starting transfers between devices  42.8 us (14%)
  other arithmetic  15.6 us (5%)
    all_to_all x1, waiting for transfers between devices, on_device(): lax.all_to_all(part_in.reshape(slot_shape + (latent_width,)), ('node', 'l...  52.2 us
    all_to_all x1, waiting for transfers between devices, on_device(): lax.all_to_all(sent_grad.reshape(slot_shape + (latent_width,)), ('node',...  31.1 us
    all_to_all x1, waiting for transfers between devices, on_device(): lax.all_to_all(sent_in.reshape(slot_shape + (latent_width,)), ('node', 'l...  30.6 us
    dot_general x1, matrix products, batched_backward(): jnp.einsum('erl,ehl->erh', rows_grad, lower, preferred_element_type=jnp.f...  13.2 us
    all_to_all x1, starting transfers between devices, on_device(): lax.all_to_all(sent_mix.reshape(slot_shape), ('node', 'local'), split_axi...  11.8 us
    dot_general x1, matrix products, batched_backward(): jnp.einsum('erh,erl->ehl', scaled, rows_grad, preferred_element_type=jnp....  11.2 us
    all_to_all x1, starting transfers between devices, on_device(): lax.all_to_all(part_in.reshape(slot_shape + (latent_width,)), ('node', 'l...  10.5 us
    select_n x1, local copies, waits for them, and re-layouts, fill_rows(): jnp.where(valid[:, None], rows_grad[token_rows], jnp.zeros((), rows_grad....  10.3 us
  transfers between devices with their start and end apart: 5, of which 3 were waited for; matrix products, arithmetic and copies ran while one was open for 29% of the time, Pallas kernels for 0%

commit v1 on v0

v1 whole, which is shorter than its diff:
```python
import functools

import jax
import jax.numpy as jnp
from jax import lax
from jax.experimental import pallas as pl
from jax.experimental.pallas import tpu as pltpu
from jax.sharding import PartitionSpec as P

F32 = jnp.float32
BF16 = jnp.bfloat16
CAP = 6
SUB = 8
NN = (((1,), (0,)), ((), ()))
NT = (((1,), (1,)), ((), ()))
TN = (((0,), (0,)), ((), ()))


def dot(a, b, dims=NN):
    return lax.dot_general(a, b, dims, preferred_element_type=F32)


def iota(shape, dim):
    return lax.broadcasted_iota(jnp.int32, shape, dim)


def ones_where(mask):
    return jnp.where(mask, 1.0, 0.0)


def pick_codes(ids_ref, mix_ref, experts):
    tokens = ids_ref.shape[1]
    e_at = iota((experts, tokens), 0)
    hit = jnp.zeros((experts, tokens), F32)
    mix = jnp.zeros((experts, tokens), F32)
    for k in range(ids_ref.shape[0]):
        named = ids_ref[k : k + 1, :] == e_at
        hit = hit + ones_where(named)
        mix = mix + jnp.where(named, mix_ref[k : k + 1, :].astype(F32), 0.0)
    earlier = ones_where(iota((tokens, tokens), 0) < iota((tokens, tokens), 1)).astype(BF16)
    code = hit * (dot(hit.astype(BF16), earlier) + 1.0)
    return code, mix


def pack_kernel(j, ids_ref, mix_ref, lat_ref, grad_ref, out_ref, code_s, mix_s):
    step = pl.program_id(0)
    experts, tokens = code_s.shape
    rows = out_ref.shape[0]

    @pl.when(step == 0)
    def _():
        code, mix = pick_codes(ids_ref, mix_ref, experts)
        code_s[...] = code.astype(BF16)
        mix_s[...] = mix.astype(BF16)

    at = iota((rows, experts), 0) + step * rows
    spread = ones_where(iota((rows, experts), 1) == 2 * (at >> 4) + j).astype(BF16)
    code = dot(spread, code_s[...]).astype(jnp.int32)
    mix = dot(spread, mix_s[...])
    s = iota((rows, tokens), 0) & 7
    lat_hit = ones_where((s < 6) & (code == s + 1))
    grad_a = jnp.where((s >= 6) & (code == s - 5), mix, 0.0)
    grad_lo = jnp.where((s < 4) & (code == s + 3), mix, 0.0)
    grad_hi = jnp.where((s >= 4) & (code == s - 1), mix, 0.0)
    half = lat_ref.shape[1] // 2
    first = jnp.concatenate([lat_hit, grad_a], axis=1).astype(BF16)
    source = jnp.concatenate([lat_ref[...], grad_ref[...]], axis=0)
    out_ref[:, : 2 * half] = dot(first, source).astype(BF16)
    second = jnp.concatenate([grad_lo, grad_hi], axis=1).astype(BF16)
    folded = jnp.concatenate([grad_ref[:, :half], grad_ref[:, half:]], axis=0)
    out_ref[:, 2 * half :] = dot(second, folded).astype(BF16)


def pack(j, ids, mix, lat, grad, experts, owners):
    tokens, width = lat.shape
    rows = owners * SUB
    steps = 4
    whole = lambda a: pl.BlockSpec(a.shape, lambda i: (0, 0))
    return pl.pallas_call(
        functools.partial(pack_kernel, j),
        grid=(steps,),
        in_specs=[whole(ids), whole(mix), whole(lat), whole(grad)],
        out_specs=pl.BlockSpec((rows // steps, 3 * width // 2), lambda i: (i, 0)),
        out_shape=jax.ShapeDtypeStruct((rows, 3 * width // 2), BF16),
        scratch_shapes=[pltpu.VMEM((experts, tokens), BF16), pltpu.VMEM((experts, tokens), BF16)],
        compiler_params=pltpu.CompilerParams(vmem_limit_bytes=24 << 20),
        cost_estimate=pl.CostEstimate(flops=2 * rows * 256 * width * 3 // 2, bytes_accessed=3 * rows * width, transcendentals=0),
        name="pack",
    )(ids, mix, lat, grad)


GROUP = 256
PICKS = GROUP // SUB * CAP


def place(shape, row_dim, rank_of_s, ok):
    other = 1 - row_dim
    pick, row = iota(shape, row_dim), iota(shape, other)
    s = row & 7
    return ones_where((pick == (row >> 3) * CAP + rank_of_s(s)) & ok(s)).astype(BF16)


def expert_kernel(recv_ref, up_ref, down_ref, x_ref, g_ref, hg_ref, sq_ref, back_ref, acc):
    step = pl.program_id(0)
    last = pl.num_programs(0) - 1
    half = x_ref.shape[1] // 2
    groups = recv_ref.shape[0] // GROUP

    @pl.when(step == 0)
    def _():
        shape = (PICKS, GROUP)
        first = jnp.concatenate(
            [
                place(shape, 0, lambda s: s, lambda s: s < 6),
                place(shape, 0, lambda s: s - 6, lambda s: s >= 6),
            ],
            axis=0,
        )
        second = jnp.concatenate(
            [
                place(shape, 0, lambda s: s + 2, lambda s: s < 4),
                place(shape, 0, lambda s: s - 2, lambda s: s >= 4),
            ],
            axis=0,
        )

        def unfold(g, carry):
            raw = pl.ds(pl.multiple_of(g * GROUP, GROUP), GROUP)
            out = pl.ds(pl.multiple_of(g * PICKS, PICKS), PICKS)
            a = dot(first, recv_ref[raw, : 2 * half])
            x_ref[out, :] = a[:PICKS].astype(BF16)
            b = dot(second, recv_ref[raw, 2 * half :])
            g_ref[out, :half] = (a[PICKS:, :half] + b[:PICKS]).astype(BF16)
            g_ref[out, half:] = (a[PICKS:, half:] + b[PICKS:]).astype(BF16)
            return carry

        lax.fori_loop(0, groups, unfold, 0)

    up = up_ref[0, 0]
    pre = dot(up, x_ref[...], NT)
    pulled = dot(down_ref[0, 0], g_ref[...], NT)
    act = jnp.maximum(pre, 0.0)
    sq_ref[...] = (act * act).astype(BF16)
    hg = (2.0 * act * pulled).astype(BF16)
    hg_ref[...] = hg
    part = dot(hg, up, TN)

    @pl.when(step == 0)
    def _():
        acc[...] = part

    @pl.when(step > 0)
    def _():
        acc[...] += part

    @pl.when(step == last)
    def _():
        quarter = half // 2
        shape = (GROUP, PICKS)
        main = place(shape, 1, lambda s: s, lambda s: s < 6)
        rest = [place(shape, 1, lambda s, b=b: s - 6 + 2 * b, lambda s: s >= 6) for b in range(3)]

        def fold(g, carry):
            raw = pl.ds(pl.multiple_of(g * GROUP, GROUP), GROUP)
            src = pl.ds(pl.multiple_of(g * PICKS, PICKS), PICKS)
            y = acc[src, :].astype(BF16)
            tail = y[:, 3 * quarter :]
            for b in range(3):
                cols = slice(b * quarter, (b + 1) * quarter)
                back_ref[raw, cols] = (dot(main, y[:, cols]) + dot(rest[b], tail)).astype(BF16)
            return carry

        lax.fori_loop(0, groups, fold, 0)


def expert_rows(j, recv, up, down, blocks=3):
    rows = recv.shape[0]
    hidden, width = up.shape[2:]
    picks = rows // SUB * CAP
    hb = hidden // blocks
    weight = pl.BlockSpec((1, 1, hb, width), lambda i: (0, j, i, 0))
    fixed = lambda shape: pl.BlockSpec(shape, lambda i: (0, 0))
    slab = pl.BlockSpec((hb, picks), lambda i: (i, 0))
    return pl.pallas_call(
        expert_kernel,
        grid=(blocks,),
        in_specs=[fixed(recv.shape), weight, weight],
        out_specs=[fixed((picks, width)), fixed((picks, width)), slab, slab, fixed((rows, 3 * width // 4))],
        out_shape=[
            jax.ShapeDtypeStruct((picks, width), BF16),
            jax.ShapeDtypeStruct((picks, width), BF16),
            jax.ShapeDtypeStruct((hidden, picks), BF16),
            jax.ShapeDtypeStruct((hidden, picks), BF16),
            jax.ShapeDtypeStruct((rows, 3 * width // 4), BF16),
        ],
        scratch_shapes=[pltpu.VMEM((picks, width), F32)],
        compiler_params=pltpu.CompilerParams(vmem_limit_bytes=48 << 20),
        cost_estimate=pl.CostEstimate(
            flops=6 * picks * hidden * width, bytes_accessed=4 * hidden * width + 4 * hidden * picks + 10 * picks * width, transcendentals=0
        ),
        name="expert_rows",
    )(recv, up, down)


def weights_kernel(hg_ref, sq_ref, x_ref, g_ref, up_ref, down_ref):
    up_ref[...] = dot(hg_ref[...], x_ref[...]).astype(BF16)
    down_ref[...] = dot(sq_ref[...], g_ref[...]).astype(BF16)


def weight_grads(hg, sq, x, g, blocks=3):
    hidden, picks = hg.shape
    width = x.shape[1]
    hb = hidden // blocks
    fixed = lambda shape: pl.BlockSpec(shape, lambda i: (0, 0))
    slab = pl.BlockSpec((hb, picks), lambda i: (i, 0))
    out = pl.BlockSpec((hb, width), lambda i: (i, 0))
    return pl.pallas_call(
        weights_kernel,
        grid=(blocks,),
        in_specs=[slab, slab, fixed((picks, width)), fixed((picks, width))],
        out_specs=[out, out],
        out_shape=[jax.ShapeDtypeStruct((hidden, width), BF16)] * 2,
        compiler_params=pltpu.CompilerParams(vmem_limit_bytes=32 << 20),
        cost_estimate=pl.CostEstimate(
            flops=4 * picks * hidden * width, bytes_accessed=4 * hidden * picks + 4 * picks * width + 4 * hidden * width, transcendentals=0
        ),
        name="weight_grads",
    )(hg, sq, x, g)


def combine_kernel(experts, ids_ref, mix_ref, lat_ref, back0_ref, back1_ref, lat_out, mix_out):
    picks, tokens = ids_ref.shape
    rows = back0_ref.shape[0]
    quarter = lat_ref.shape[1] // 4
    code, _ = pick_codes(ids_ref, mix_ref, experts)
    code = code.astype(BF16)
    s = iota((tokens, rows), 1) & 7
    total = jnp.zeros((tokens, 3 * quarter), F32)
    total_tail = jnp.zeros((tokens, quarter), F32)
    gained = jnp.zeros((experts, tokens), F32)
    for j, back_ref in enumerate((back0_ref, back1_ref)):
        spread = ones_where(iota((experts, rows), 0) == 2 * (iota((experts, rows), 1) >> 4) + j).astype(BF16)
        here = dot(code, spread, TN).astype(jnp.int32)
        main = ones_where((s < 6) & (here == s + 1))
        back = back_ref[...]
        total = total + dot(main.astype(BF16), back)
        dots = main * dot(lat_ref[:, : 3 * quarter], back, NT)
        for b in range(3):
            rest = ones_where((s >= 6) & (here == s - 5 + 2 * b))
            part = back[:, b * quarter : (b + 1) * quarter]
            total_tail = total_tail + dot(rest.astype(BF16), part)
            dots = dots + rest * dot(lat_ref[:, 3 * quarter :], part, NT)
        high = dots.astype(BF16)
        low = (dots - high.astype(F32)).astype(BF16)
        gained = gained + dot(spread, high, NT) + dot(spread, low, NT)
    lat_out[:, : 3 * quarter] = total.astype(BF16)
    lat_out[:, 3 * quarter :] = total_tail.astype(BF16)
    e_at = iota((experts, tokens), 0)
    for k in range(picks):
        dots = jnp.sum(jnp.where(ids_ref[k : k + 1, :] == e_at, gained, 0.0), axis=0, keepdims=True)
        mix_out[k : k + 1, :] = dots / (2.0 * mix_ref[k : k + 1, :].astype(F32))


def combine_back(ids, mix, lat, back0, back1, experts):
    picks, tokens = ids.shape
    return pl.pallas_call(
        functools.partial(combine_kernel, experts),
        out_shape=[jax.ShapeDtypeStruct(lat.shape, BF16), jax.ShapeDtypeStruct((picks, tokens), F32)],
        compiler_params=pltpu.CompilerParams(vmem_limit_bytes=32 << 20),
        name="combine_back",
    )(ids, mix, lat, back0, back1)


AXES = ("node", "local")


def exchange(rows, owners):
    shape = rows.shape
    moved = lax.all_to_all(rows.reshape(owners, SUB, shape[1]), AXES, split_axis=0, concat_axis=0, tiled=True)
    return moved.reshape(shape)


def on_device(latent, grad_out, expert_ids, combine, w_up, w_down):
    owners = lax.axis_size("node") * lax.axis_size("local")
    exp_local = w_up.shape[1]
    experts = owners // 2 * exp_local
    ids, mix = expert_ids.T, combine.T
    up = jnp.swapaxes(w_up, 2, 3)
    backs, d_up, d_down = [], [], []
    for j in range(exp_local):
        recv = exchange(pack(j, ids, mix, latent, grad_out, experts, owners), owners)
        x, g, hg, sq, back = expert_rows(j, recv, up, w_down)
        backs.append(exchange(back, owners))
        du, dv = weight_grads(hg, sq, x, g)
        d_up.append(du)
        d_down.append(dv)
    lat_grad, mix_grad = combine_back(ids, mix, latent, *backs, experts)
    return (
        lat_grad,
        mix_grad.T,
        jnp.swapaxes(jnp.stack(d_up), 1, 2)[None],
        jnp.stack(d_down)[None],
    )


def solution(mesh):
    in_specs = (
        P(AXES, None),
        P(AXES, None),
        P(AXES, None),
        P(AXES, None),
        P(AXES, None, None, None),
        P(AXES, None, None, None),
    )
    out_specs = (
        P(AXES, None),
        P(AXES, None),
        P(AXES, None, None, None),
        P(AXES, None, None, None),
    )
    return jax.shard_map(
        on_device, mesh=mesh, in_specs=in_specs, out_specs=out_specs, check_vma=False
    )
```

time: 303 us -> 170 us (0.56); the launches traced: 298 us -> 169 us
  local copies, waits for them, and re-layouts: 74.4 us -> 16.7 us
  Pallas kernels: 0 us -> 52.8 us
  matrix products: 50.5 us -> 0 us
  waiting for transfers between devices: 114 us -> 68.9 us
  starting transfers between devices: 42.8 us -> 25.7 us
  other arithmetic: 15.6 us -> 4.49 us
    pallas_call x0 -> x7, Pallas kernels: none -> 52.8 us  [the longest x2 31.8 us: expert_rows(): pl.pallas_call(expert_kernel, grid=(blocks,), in_specs=[fixed(recv.shape)...]
    dot_general x5 -> x0, matrix products: 50.5 us -> none  [the longest x1 13.2 us: batched_backward(): jnp.einsum('erl,ehl->erh', rows_grad, lower, preferred_element_type=jnp.f...]
    all_to_all x5 -> x4, waiting for transfers between devices: 114 us -> 68.9 us  [exchange(): lax.all_to_all(rows.reshape(owners, SUB, shape[1]), AXES, split_axis=0, c...]
    gather x7 -> x0, local copies, waits for them, and re-layouts: 30.5 us -> none  [the longest x1 9.46 us: fill_rows(): mix_rows.reshape(-1)[safe]]
    select_n x2 -> x0, local copies, waits for them, and re-layouts: 18.3 us -> none  [the longest x1 10.3 us: fill_rows(): jnp.where(valid[:, None], rows_grad[token_rows], jnp.zeros((), rows_grad....]
    all_to_all x5 -> x4, starting transfers between devices: 42.8 us -> 25.7 us  [exchange(): lax.all_to_all(rows.reshape(owners, SUB, shape[1]), AXES, split_axis=0, c...]
    unnamed x14 -> x44, local copies, waits for them, and re-layouts: 2.33 us -> 16.7 us
    reduce_sum x4 -> x0, other arithmetic: 9.96 us -> none  [the longest x1 7.52 us: on_device(): rows_back = back_in.reshape(exp_local, owner_count // 2, 2, cap_slots, la...]
  transfers between devices with their start and end apart: 5 -> 4, of which waited for: 3 -> 4; matrix products, arithmetic and copies ran while one was open for 29% -> 3% of each run, Pallas kernels for 0% -> 27%
where the time goes in v1:
time: 170 us; the launch traced here: 169 us
  waiting for transfers between devices  68.9 us (41%)
  Pallas kernels  52.8 us (31%)
  starting transfers between devices  25.7 us (15%)
  local copies, waits for them, and re-layouts  16.7 us (10%)
  other arithmetic  4.49 us (3%)
    all_to_all x4, waiting for transfers between devices, exchange(): lax.all_to_all(rows.reshape(owners, SUB, shape[1]), AXES, split_axis=0, c...  68.9 us
    pallas_call x2, Pallas kernels, expert_rows(): pl.pallas_call(expert_kernel, grid=(blocks,), in_specs=[fixed(recv.shape)...  31.8 us
    all_to_all x4, starting transfers between devices, exchange(): lax.all_to_all(rows.reshape(owners, SUB, shape[1]), AXES, split_axis=0, c...  25.7 us
    unnamed x44, local copies, waits for them, and re-layouts  16.7 us
    pallas_call x2, Pallas kernels, weight_grads(): pl.pallas_call(weights_kernel, grid=(blocks,), in_specs=[slab, slab, fixe...  9.62 us
    pallas_call x2, Pallas kernels, pack(): pl.pallas_call(functools.partial(pack_kernel, j), grid=(steps,), in_specs...  6.94 us
    broadcast_in_dim x1, other arithmetic, on_device(): jnp.swapaxes(jnp.stack(d_up), 1, 2)[None]  4.49 us
    pallas_call x1, Pallas kernels, combine_back(): pl.pallas_call(functools.partial(combine_kernel, experts), out_shape=[jax...  4.43 us
  transfers between devices with their start and end apart: 4, of which 4 were waited for; matrix products, arithmetic and copies ran while one was open for 3% of the time, Pallas kernels for 27%

profile of v1, /device:TPU:1, one launch (start us, length us, event | category | flops | bytes accessed | tf_op | source)
XLA Modules:
  0.0 169.4 jit_solution(18224391927872463400)
XLA Ops:
  0.6 0.0 copy-start
  0.6 0.9 copy-done
  1.6 0.0 copy-start.3
  1.6 0.9 copy-done.3
  2.5 0.0 copy-start.5
  2.5 0.7 copy-done.5
  3.2 0.0 copy-start.7
  3.2 0.7 copy-done.7
  3.9 3.5 %pack.2 = bf16[1024,1536]{1,0:T(8,128)(2,1)} custom-call(s32[4,128]{1,0:T(4,128)S(1)} %bitcast.29, bf16[4,128]{1,0:T(4,128)(2,1)S(1)} %bitcast.32, bf16[128,1024]{1,0:T(8,128)(2,1)S(1)} %copy-done, bf16[128,1024]{1,0:T(8,128)(2,1)S(1)} %copy-done.3), custom_call_target="tpu_custom_call" | custom-call | flops 805306368 | bytes 3145728 | tf_op jit(solution)/shard_map/pack/pallas_call | solution.py:79
  7.4 0.0 copy-start.1
  7.4 0.0 copy-start.4
  7.4 0.0 copy-start.8
  7.4 11.9 %all-to-all-start = ((bf16[128,8,1536]{2,1,0:T(8,128)(2,1)}), bf16[128,8,1536]{2,1,0:T(8,128)(2,1)}, u32[]{:S(2)}, u32[]{:S(2)}) async-start(bf16[128,8,1536]{2,1,0:T(8,128)(2,1)} %bitcast.2), calls=%async_computation | async-start | bytes 6291456 | tf_op jit(solution)/shard_map/all_to_all | solution.py:279
  19.3 0.0 copy-done.1
  19.3 0.0 copy-done.4
  19.3 0.0 copy-done.6
  19.3 0.0 copy-done.8
  19.3 3.5 %pack.3 = bf16[1024,1536]{1,0:T(8,128)(2,1)} custom-call(s32[4,128]{1,0:T(4,128)S(1)} %bitcast.30, bf16[4,128]{1,0:T(4,128)(2,1)S(1)} %bitcast.33, bf16[128,1024]{1,0:T(8,128)(2,1)S(1)} %copy-done.1, bf16[128,1024]{1,0:T(8,128)(2,1)S(1)} %copy-done.4), custom_call_target="tpu_custom_call" | custom-call | flops 805306368 | bytes 3145728 | tf_op jit(solution)/shard_map/pack/pallas_call | solution.py:79
  22.8 37.2 %all-to-all-done = bf16[128,8,1536]{2,1,0:T(8,128)(2,1)} async-done(((bf16[128,8,1536]{2,1,0:T(8,128)(2,1)}), bf16[128,8,1536]{2,1,0:T(8,128)(2,1)}, u32[]{:S(2)}, u32[]{:S(2)}) %all-to-all-start) | async-done | bytes 3145760 | tf_op jit(solution)/shard_map/all_to_all | solution.py:279
  60.0 4.5 %all-to-all-start.2 = ((bf16[128,8,1536]{2,1,0:T(8,128)(2,1)}), bf16[128,8,1536]{2,1,0:T(8,128)(2,1)S(1)}, u32[]{:S(2)}, u32[]{:S(2)}) async-start(bf16[128,8,1536]{2,1,0:T(8,128)(2,1)} %bitcast.7), calls=%async_computation.2 | async-start | bytes 6291456 | tf_op jit(solution)/shard_map/all_to_all | solution.py:279
  64.5 16.2 %expert_rows.2 = (bf16[768,1024]{1,0:T(8,128)(2,1)S(1)}, bf16[768,1024]{1,0:T(8,128)(2,1)S(1)}, bf16[1344,768]{1,0:T(8,128)(2,1)}, bf16[1344,768]{1,0:T(8,128)(2,1)}, bf16[1024,768]{1,0:T(8,128)(2,1)}) custom-call(bf16[1024,1536]{1,0:T(8,128)(2,1)} %bitcast.3.recv_ref, bf16[1,2,1344,1024]{3,2,1,0:T(8,128)(2,1)} %bitcast.36, bf16[1,2,1344,1024]{3,2,1,0:T(8,128)(2,1)} %down_ref.3), custom_call_target="tpu_custom_call" | custom-call | flops 6341787648 | bytes 17498112 | tf_op jit(solution)/shard_map/expert_rows/pallas_call | solution.py:184
  80.7 0.0 copy-start.13
  80.7 1.1 copy-done.13
  81.8 0.0 copy-start.15
  81.8 1.2 copy-done.15
  83.0 22.5 %all-to-all-done.2 = bf16[128,8,1536]{2,1,0:T(8,128)(2,1)S(1)} async-done(((bf16[128,8,1536]{2,1,0:T(8,128)(2,1)}), bf16[128,8,1536]{2,1,0:T(8,128)(2,1)S(1)}, u32[]{:S(2)}, u32[]{:S(2)}) %all-to-all-start.2) | async-done | bytes 3145760 | tf_op jit(solution)/shard_map/all_to_all | solution.py:279
  105.5 1.7 copy-done.21
  107.2 4.5 %all-to-all-start.1 = ((bf16[128,8,768]{2,1,0:T(8,128)(2,1)}), bf16[128,8,768]{2,1,0:T(8,128)(2,1)S(1)}, u32[]{:S(2)}, u32[]{:S(2)}) async-start(bf16[128,8,768]{2,1,0:T(8,128)(2,1)} %bitcast.5), calls=%async_computation.1 | async-start | bytes 3145728 | tf_op jit(solution)/shard_map/all_to_all | solution.py:279
  111.7 15.6 %expert_rows.3 = (bf16[768,1024]{1,0:T(8,128)(2,1)S(1)}, bf16[768,1024]{1,0:T(8,128)(2,1)S(1)}, bf16[1344,768]{1,0:T(8,128)(2,1)}, bf16[1344,768]{1,0:T(8,128)(2,1)}, bf16[1024,768]{1,0:T(8,128)(2,1)S(1)}) custom-call(bf16[1024,1536]{1,0:T(8,128)(2,1)} %bitcast.35, bf16[1,2,1344,1024]{3,2,1,0:T(8,128)(2,1)} %bitcast.37, bf16[1,2,1344,1024]{3,2,1,0:T(8,128)(2,1)} %down_ref.3), custom_call_target="tpu_custom_call" | custom-call | flops 6341787648 | bytes 17498112 | tf_op jit(solution)/shard_map/expert_rows/pallas_call | solution.py:184
  127.3 1.1 copy-done.2
  128.5 1.1 copy-done.17
  129.6 1.2 copy-done.19
  130.8 5.1 %all-to-all-done.1 = bf16[128,8,768]{2,1,0:T(8,128)(2,1)S(1)} async-done(((bf16[128,8,768]{2,1,0:T(8,128)(2,1)}), bf16[128,8,768]{2,1,0:T(8,128)(2,1)S(1)}, u32[]{:S(2)}, u32[]{:S(2)}) %all-to-all-start.1) | async-done | bytes 1572896 | tf_op jit(solution)/shard_map/all_to_all | solution.py:279
  135.8 4.8 %all-to-all-start.3 = ((bf16[128,8,768]{2,1,0:T(8,128)(2,1)}), bf16[128,8,768]{2,1,0:T(8,128)(2,1)S(1)}, u32[]{:S(2)}, u32[]{:S(2)}) async-start(bf16[128,8,768]{2,1,0:T(8,128)(2,1)} %bitcast.28), calls=%async_computation.3 | async-start | bytes 3145728 | tf_op jit(solution)/shard_map/all_to_all | solution.py:279
  140.7 0.0 copy-start.9
  140.7 1.6 copy-done.9
  142.2 1.6 copy-done.10
  143.8 1.4 copy-done.14
  145.2 1.4 copy-done.16
  146.7 4.8 %weight_grads.2 = (bf16[1344,1024]{1,0:T(8,128)(2,1)S(1)}, bf16[1344,1024]{1,0:T(8,128)(2,1)S(1)}) custom-call(bf16[1344,768]{1,0:T(8,128)(2,1)S(1)} %copy-done.9, bf16[1344,768]{1,0:T(8,128)(2,1)S(1)} %copy-done.10, bf16[768,1024]{1,0:T(8,128)(2,1)S(1)} %copy-done.14, bf16[768,1024]{1,0:T(8,128)(2,1)S(1)} %copy-done.16), custom_call_target="tpu_custom_call" | custom-call | flops 4227858432 | bytes 12779520 | tf_op jit(solution)/shard_map/weight_grads/pallas_call | solution.py:217
  151.5 0.0 copy-done.11
  151.5 0.0 copy-done.12
  151.5 0.0 copy-done.18
  151.5 0.0 copy-done.20
  151.5 4.8 %weight_grads.3 = (bf16[1344,1024]{1,0:T(8,128)(2,1)S(1)}, bf16[1344,1024]{1,0:T(8,128)(2,1)S(1)}) custom-call(bf16[1344,768]{1,0:T(8,128)(2,1)S(1)} %copy-done.11, bf16[1344,768]{1,0:T(8,128)(2,1)S(1)} %copy-done.12, bf16[768,1024]{1,0:T(8,128)(2,1)S(1)} %copy-done.18, bf16[768,1024]{1,0:T(8,128)(2,1)S(1)} %copy-done.20), custom_call_target="tpu_custom_call" | custom-call | flops 4227858432 | bytes 12779520 | tf_op jit(solution)/shard_map/weight_grads/pallas_call | solution.py:217
  156.3 4.5 %maximum_bitcast_fusion = (bf16[1,2,1024,1344]{2,3,1,0:T(8,128)(2,1)}, bf16[1,2,1344,1024]{3,2,1,0:T(8,128)(2,1)}) fusion(bf16[1,1344,1024]{2,1,0:T(8,128)(2,1)S(1)} %bitcast.26, bf16[1,1344,1024]{2,1,0:T(8,128)(2,1)S(1)} %bitcast.24, bf16[1,1344,1024]{2,1,0:T(8,128)(2,1)S(1)} %bitcast.27, bf16[1,1344,1024]{2,1,0:T(8,128)(2,1)S(1)} %bitcast.25), kind=kLoop, calls=%fused_computation | loop fusion | flops 5505024 | bytes 22020096 | tf_op jit(solution)/shard_map/broadcast_in_dim | solution.py:301
  160.8 4.1 %all-to-all-done.3 = bf16[128,8,768]{2,1,0:T(8,128)(2,1)S(1)} async-done(((bf16[128,8,768]{2,1,0:T(8,128)(2,1)}), bf16[128,8,768]{2,1,0:T(8,128)(2,1)S(1)}, u32[]{:S(2)}, u32[]{:S(2)}) %all-to-all-start.3) | async-done | bytes 1572896 | tf_op jit(solution)/shard_map/all_to_all | solution.py:279
  164.9 4.4 %combine_back.1 = (bf16[128,1024]{1,0:T(8,128)(2,1)}, f32[4,128]{1,0:T(4,128)}) custom-call(s32[4,128]{1,0:T(4,128)S(1)} %bitcast.31, bf16[4,128]{1,0:T(4,128)(2,1)S(1)} %bitcast.34, bf16[128,1024]{1,0:T(8,128)(2,1)S(1)} %copy-done.1, bf16[1024,768]{1,0:T(8,128)(2,1)S(1)} %bitcast.22, bf16[1024,768]{1,0:T(8,128)(2,1)S(1)} %bitcast.23), custom_call_target="tpu_custom_call" | custom-call | tf_op jit(solution)/shard_map/combine_back/pallas_call | solution.py:266
  (12 shorter events, 0.0 us)
Async XLA Ops:
  0.6 1.0 copy-start
  1.6 0.9 copy-start.3
  2.5 0.7 copy-start.5
  3.2 0.7 copy-start.7
  7.4 11.9 %copy-start.1 = (bf16[128,1024]{1,0:T(8,128)(2,1)S(1)}, bf16[128,1024]{1,0:T(8,128)(2,1)}, u32[]{:S(2)}) copy-start(bf16[128,1024]{1,0:T(8,128)(2,1)} %lat_ref.5) | copy-start | bytes 786436
  7.4 11.9 %copy-start.4 = (bf16[128,1024]{1,0:T(8,128)(2,1)S(1)}, bf16[128,1024]{1,0:T(8,128)(2,1)}, u32[]{:S(2)}) copy-start(bf16[128,1024]{1,0:T(8,128)(2,1)} %grad_ref.3) | copy-start | bytes 786436
  7.4 11.9 %copy-start.6 = (s32[128,4]{0,1:T(4,128)S(1)}, s32[128,4]{0,1:T(4,128)}, u32[]{:S(2)}) copy-start(s32[128,4]{0,1:T(4,128)} %param.8) | copy-start | bytes 6148
  7.4 11.9 %copy-start.8 = (bf16[128,4]{0,1:T(4,128)(2,1)S(1)}, bf16[128,4]{0,1:T(4,128)(2,1)}, u32[]{:S(2)}) copy-start(bf16[128,4]{0,1:T(4,128)(2,1)} %param.9) | copy-start | bytes 3076
  7.4 52.7 %all-to-all-start = ((bf16[128,8,1536]{2,1,0:T(8,128)(2,1)}), bf16[128,8,1536]{2,1,0:T(8,128)(2,1)}, u32[]{:S(2)}, u32[]{:S(2)}) async-start(bf16[128,8,1536]{2,1,0:T(8,128)(2,1)} %bitcast.2), calls=%async_computation | async-start | bytes 6291456 | tf_op jit(solution)/shard_map/all_to_all | solution.py:279
  60.0 45.5 %all-to-all-start.2 = ((bf16[128,8,1536]{2,1,0:T(8,128)(2,1)}), bf16[128,8,1536]{2,1,0:T(8,128)(2,1)S(1)}, u32[]{:S(2)}, u32[]{:S(2)}) async-start(bf16[128,8,1536]{2,1,0:T(8,128)(2,1)} %bitcast.7), calls=%async_computation.2 | async-start | bytes 6291456 | tf_op jit(solution)/shard_map/all_to_all | solution.py:279
  80.7 1.1 copy-start.13
  81.8 1.2 copy-start.15
  105.5 1.7 copy-start.21
  107.2 28.6 %all-to-all-start.1 = ((bf16[128,8,768]{2,1,0:T(8,128)(2,1)}), bf16[128,8,768]{2,1,0:T(8,128)(2,1)S(1)}, u32[]{:S(2)}, u32[]{:S(2)}) async-start(bf16[128,8,768]{2,1,0:T(8,128)(2,1)} %bitcast.5), calls=%async_computation.1 | async-start | bytes 3145728 | tf_op jit(solution)/shard_map/all_to_all | solution.py:279
  127.3 1.1 copy-start.2
  128.5 1.1 copy-start.17
  129.6 1.2 copy-start.19
  135.8 29.1 %all-to-all-start.3 = ((bf16[128,8,768]{2,1,0:T(8,128)(2,1)}), bf16[128,8,768]{2,1,0:T(8,128)(2,1)S(1)}, u32[]{:S(2)}, u32[]{:S(2)}) async-start(bf16[128,8,768]{2,1,0:T(8,128)(2,1)} %bitcast.28), calls=%async_computation.3 | async-start | bytes 3145728 | tf_op jit(solution)/shard_map/all_to_all | solution.py:279
  140.7 1.6 copy-start.9
  142.2 1.6 copy-start.10
  143.8 1.4 copy-start.14
  145.2 1.4 copy-start.16
  146.6 4.8 %copy-start.11 = (bf16[1344,768]{1,0:T(8,128)(2,1)S(1)}, bf16[1344,768]{1,0:T(8,128)(2,1)}, u32[]{:S(2)}) copy-start(bf16[1344,768]{1,0:T(8,128)(2,1)} %get-tuple-element.29.hg_ref) | copy-start | bytes 6193156
  146.6 4.8 %copy-start.12 = (bf16[1344,768]{1,0:T(8,128)(2,1)S(1)}, bf16[1344,768]{1,0:T(8,128)(2,1)}, u32[]{:S(2)}) copy-start(bf16[1344,768]{1,0:T(8,128)(2,1)} %get-tuple-element.30.sq_ref) | copy-start | bytes 6193156
  146.6 4.8 %copy-start.18 = (bf16[768,1024]{1,0:T(8,128)(2,1)S(1)}, bf16[768,1024]{1,0:T(8,128)(2,1)}, u32[]{:S(2)}) copy-start(bf16[768,1024]{1,0:T(8,128)(2,1)} %copy-done.17) | copy-start | bytes 4718596
  146.6 4.9 %copy-start.20 = (bf16[768,1024]{1,0:T(8,128)(2,1)S(1)}, bf16[768,1024]{1,0:T(8,128)(2,1)}, u32[]{:S(2)}) copy-start(bf16[768,1024]{1,0:T(8,128)(2,1)} %copy-done.19) | copy-start | bytes 4718596

commit v2 on v0

v2 whole, which is shorter than its diff:
```python
import functools

import jax
import jax.numpy as jnp
from jax import lax
from jax.experimental import pallas as pl
from jax.experimental.pallas import tpu as pltpu
from jax.sharding import PartitionSpec as P

F32 = jnp.float32
BF16 = jnp.bfloat16
CAP = 6
SUB = 8
GROUP = 256
MIB = 1 << 20
NN = (((1,), (0,)), ((), ()))
NT = (((1,), (1,)), ((), ()))
TN = (((0,), (0,)), ((), ()))
AXES = ("node", "local")
IN_HBM = pl.BlockSpec(memory_space=pltpu.HBM)


def dot(a, b, dims=NN):
    return lax.dot_general(a, b, dims, preferred_element_type=F32)


def iota(shape, dim):
    return lax.broadcasted_iota(jnp.int32, shape, dim)


def one_hot(mask):
    return jnp.where(mask, 1.0, 0.0).astype(BF16)


def pick_codes(ids, mix, experts):
    tokens = ids.shape[1]
    e_at = iota((experts, tokens), 0)
    hit = jnp.zeros((experts, tokens), F32)
    weight = jnp.zeros((experts, tokens), F32)
    for k in range(ids.shape[0]):
        named = ids[k : k + 1, :] == e_at
        hit = hit + jnp.where(named, 1.0, 0.0)
        weight = weight + jnp.where(named, mix[k : k + 1, :], 0.0)
    earlier = one_hot(iota((tokens, tokens), 0) < iota((tokens, tokens), 1))
    code = hit * (dot(hit.astype(BF16), earlier) + 1.0)
    return code.astype(BF16), weight.astype(BF16)


def slot_masks(code0, code1, s):
    main = jnp.where(s < CAP, code0 - 1, code1 + (CAP - 1)) == s
    main = main & (jnp.where(s < CAP, code0, code1) > 0)
    return main, (s < 4) & (code1 == s + 3), (s >= 4) & (code1 == s - 1)


def pack_kernel(ids_ref, mix_ref, lat_hbm, grad_hbm, out_ref, code_s, weight_s, both_s, sems):
    step = pl.program_id(0)
    experts, tokens = code_s.shape
    rows, width = out_ref.shape[0], lat_hbm.shape[1]

    @pl.when(step == 0)
    def _():
        one = pltpu.make_async_copy(lat_hbm, both_s.at[pl.ds(0, tokens)], sems.at[0])
        two = pltpu.make_async_copy(grad_hbm, both_s.at[pl.ds(tokens, tokens)], sems.at[1])
        one.start()
        two.start()
        code, weight = pick_codes(ids_ref[...], mix_ref[...].astype(F32), experts)
        code_s[...] = code
        weight_s[...] = weight
        one.wait()
        two.wait()

    at = (iota((rows, experts), 0) + step * rows) >> 4
    e_at = iota((rows, experts), 1)
    even, odd = one_hot(e_at == 2 * at), one_hot(e_at == 2 * at + 1)
    s = iota((rows, tokens), 0) & 7
    code0 = dot(even, code_s[...]).astype(jnp.int32)
    code1 = dot(odd, code_s[...]).astype(jnp.int32)
    weight0, weight1 = dot(even, weight_s[...]), dot(odd, weight_s[...])
    main, low, high = slot_masks(code0, code1, s)
    out_ref[:, :width] = dot(one_hot(main), both_s[:tokens, :]).astype(BF16)
    mixed = jnp.where(main, jnp.where(s < CAP, weight0, weight1), 0.0).astype(BF16)
    out_ref[:, width : 2 * width] = dot(mixed, both_s[tokens:, :]).astype(BF16)
    rest = jnp.concatenate([jnp.where(low, 1.0, 0.0), jnp.where(high, weight1, 0.0)], axis=1)
    out_ref[:, 2 * width :] = dot(rest.astype(BF16), both_s[...]).astype(BF16)


def pack(ids, mix, lat, grad, experts, owners):
    tokens, width = lat.shape
    rows, steps = owners * SUB, 4
    whole = lambda a: pl.BlockSpec(a.shape, lambda i: (0, 0))
    return pl.pallas_call(
        pack_kernel,
        grid=(steps,),
        in_specs=[whole(ids), whole(mix), IN_HBM, IN_HBM],
        out_specs=pl.BlockSpec((rows // steps, 3 * width), lambda i: (i, 0)),
        out_shape=jax.ShapeDtypeStruct((rows, 3 * width), BF16),
        scratch_shapes=[
            pltpu.VMEM((experts, tokens), BF16),
            pltpu.VMEM((experts, tokens), BF16),
            pltpu.VMEM((2 * tokens, width), BF16),
            pltpu.SemaphoreType.DMA((2,)),
        ],
        compiler_params=pltpu.CompilerParams(vmem_limit_bytes=60 * MIB),
        cost_estimate=pl.CostEstimate(flops=8 * rows * tokens * width, bytes_accessed=6 * rows * width, transcendentals=0),
        name="pack",
    )(ids, mix, lat, grad)


def slot_order(shape, pick_dim, tail):
    pick, row = iota(shape, pick_dim), iota(shape, 1 - pick_dim)
    source, s = row >> 3, row & 7
    if tail:
        half = GROUP // 2
        return one_hot(pick == jnp.where(s < 4, source * 4 + s, half + source * 4 + s - 4))
    first = GROUP // SUB * CAP
    return one_hot(pick == jnp.where(s < CAP, source * CAP + s, first + source * 2 + s - CAP))


def rows_kernel(
    recv_hbm, up_hbm, down_hbm, x_hbm, g_hbm, hg_hbm, sq_hbm, back_hbm,
    recv_s, up_s, down_s, x_s, g_s, hg_s, sq_s, y_s, back_s, recv_sems, sems, back_sems,
):
    exp_local, hidden, width = up_s.shape
    half, quarter = width // 2, GROUP // 2
    groups = recv_s.shape[0] // GROUP
    picks = x_s.shape[1]
    first = GROUP // SUB * CAP
    second = GROUP - first
    square = (GROUP, GROUP)
    kept = ((x_s, x_hbm), (g_s, g_hbm), (hg_s, hg_hbm), (sq_s, sq_hbm))

    def keep(which, j):
        scratch, hbm = kept[which]
        return pltpu.make_async_copy(scratch.at[j], hbm.at[j], sems.at[which, j])

    def load_rows(i):
        raw = pl.ds(pl.multiple_of(i * GROUP, GROUP), GROUP)
        return pltpu.make_async_copy(recv_hbm.at[raw], recv_s.at[raw], recv_sems.at[i])

    def load_up(j):
        return pltpu.make_async_copy(up_hbm.at[0, j], up_s.at[j], sems.at[4, j])

    def load_down(j):
        return pltpu.make_async_copy(down_hbm.at[0, j], down_s.at[j], sems.at[5, j])

    for i in range(groups):
        load_rows(i).start()
    for j in range(exp_local):
        load_up(j).start()
        load_down(j).start()

    take, take_tail = slot_order(square, 0, False), slot_order(square, 0, True)

    def unfold(i, carry):
        load_rows(i).wait()
        raw = pl.ds(pl.multiple_of(i * GROUP, GROUP), GROUP)
        at = pl.multiple_of(i * first, second)
        whole, head, tail = pl.ds(at, first), pl.ds(at, second), pl.ds(at + second, quarter)
        for to, cols in ((x_s, slice(0, width)), (g_s, slice(width, 2 * width))):
            moved = dot(take, recv_s[raw, cols]).astype(BF16)
            to[0, whole, :] = moved[:first]
            to[1, head, :] = moved[first:]
        moved = dot(take_tail, recv_s[raw, 2 * width :]).astype(BF16)
        x_s[1, tail, :] = moved[:quarter]
        g_s[1, tail, :] = moved[quarter:]
        return carry

    lax.fori_loop(0, groups, unfold, 0)
    for j in range(exp_local):
        keep(0, j).start()
        keep(1, j).start()

    block, tile = hidden // 3, 256
    for j in range(exp_local):
        load_up(j).wait()
        load_down(j).wait()

        def forward(i, carry):
            at = pl.ds(pl.multiple_of(i * block, 64), block)
            pre = dot(up_s[j, at, :], x_s[j], NT)
            pulled = dot(down_s[j, at, :], g_s[j], NT)
            act = jnp.maximum(pre, 0.0)
            sq_s[j, at, :] = (act * act).astype(BF16)
            hg_s[j, at, :] = (2.0 * act * pulled).astype(BF16)
            return carry

        lax.fori_loop(0, 3, forward, 0)
        keep(2, j).start()
        keep(3, j).start()
        for c in range(picks // tile):
            cols = slice(c * tile, (c + 1) * tile)
            y_s[j, cols, :] = dot(hg_s[j, :, cols], up_s[j], TN).astype(BF16)

    put, put_tail = slot_order(square, 1, False), slot_order(square, 1, True)

    def copy_out(i):
        raw = pl.ds(pl.multiple_of(i * GROUP, GROUP), GROUP)
        return pltpu.make_async_copy(back_s.at[raw], back_hbm.at[raw], back_sems.at[i])

    def fold(i, carry):
        raw = pl.ds(pl.multiple_of(i * GROUP, GROUP), GROUP)
        at = pl.multiple_of(i * first, second)
        whole, head, tail = pl.ds(at, first), pl.ds(at, second), pl.ds(at + second, quarter)
        main = jnp.concatenate([y_s[0, whole, :], y_s[1, head, :]], axis=0)
        back_s[raw, :width] = dot(put, main).astype(BF16)
        rest = jnp.concatenate([y_s[1, tail, :half], y_s[1, tail, half:]], axis=0)
        back_s[raw, width:] = dot(put_tail, rest).astype(BF16)
        copy_out(i).start()
        return carry

    lax.fori_loop(0, groups, fold, 0)
    for i in range(groups):
        copy_out(i).wait()
    for which in range(4):
        for j in range(exp_local):
            keep(which, j).wait()


def expert_rows(recv, up, down):
    rows = recv.shape[0]
    _, exp_local, hidden, width = up.shape
    picks = rows // SUB * CAP
    kept = [(exp_local, picks, width)] * 2 + [(exp_local, hidden, picks)] * 2
    back = (rows, 3 * width // 2)
    return pl.pallas_call(
        rows_kernel,
        in_specs=[IN_HBM] * 3,
        out_specs=[IN_HBM] * 5,
        out_shape=[pltpu.HBM(shape, BF16) for shape in kept + [back]],
        scratch_shapes=[pltpu.VMEM(shape, BF16) for shape in [recv.shape, up.shape[1:], up.shape[1:]] + kept + [kept[0], back]]
        + [pltpu.SemaphoreType.DMA(n) for n in ((rows // GROUP,), (6, exp_local), (rows // GROUP,))],
        compiler_params=pltpu.CompilerParams(vmem_limit_bytes=56 * MIB),
        cost_estimate=pl.CostEstimate(flops=6 * exp_local * picks * hidden * width, bytes_accessed=32 * MIB, transcendentals=0),
        name="expert_rows",
    )(recv, up, down)


def weights_kernel(experts, ids_ref, mix_ref, hg_ref, sq_ref, x_ref, g_ref, up_ref, down_ref, masks_ref, spread_ref):
    up_ref[0] = dot(hg_ref[0], x_ref[0]).astype(BF16)
    down_ref[0] = dot(sq_ref[0], g_ref[0]).astype(BF16)

    @pl.when((pl.program_id(0) == 0) & (pl.program_id(1) == 0))
    def _():
        tokens, rows = masks_ref.shape[1:]
        code, _ = pick_codes(ids_ref[...], mix_ref[...].astype(F32), experts)
        s = iota((tokens, rows), 1) & 7
        e_at, pair = iota((experts, rows), 0), 2 * (iota((experts, rows), 1) >> 4)
        even, odd = one_hot(e_at == pair), one_hot(e_at == pair + 1)
        code0 = dot(code, even, TN).astype(jnp.int32)
        code1 = dot(code, odd, TN).astype(jnp.int32)
        for i, mask in enumerate(slot_masks(code0, code1, s)):
            masks_ref[i] = one_hot(mask)
        spread_ref[0] = jnp.where((iota((experts, rows), 1) & 7) < CAP, even, odd)
        spread_ref[1] = odd


def weight_grads(ids, mix, hg, sq, x, g, experts, blocks=3):
    exp_local, hidden, picks = hg.shape
    width = x.shape[2]
    tokens, rows = ids.shape[1], picks // CAP * SUB
    hb = hidden // blocks
    whole = lambda a: pl.BlockSpec(a.shape, lambda j, i: (0,) * a.ndim)
    slab = pl.BlockSpec((1, hb, picks), lambda j, i: (j, i, 0))
    per_expert = pl.BlockSpec((1, picks, width), lambda j, i: (j, 0, 0))
    out = pl.BlockSpec((1, hb, width), lambda j, i: (j, i, 0))
    fixed = lambda n, m: pl.BlockSpec((n, m, rows), lambda j, i: (0, 0, 0))
    return pl.pallas_call(
        functools.partial(weights_kernel, experts),
        grid=(exp_local, blocks),
        in_specs=[whole(ids), whole(mix), slab, slab, per_expert, per_expert],
        out_specs=[out, out, fixed(3, tokens), fixed(2, experts)],
        out_shape=[jax.ShapeDtypeStruct((exp_local, hidden, width), BF16)] * 2
        + [pltpu.HBM((3, tokens, rows), BF16), pltpu.HBM((2, experts, rows), BF16)],
        compiler_params=pltpu.CompilerParams(vmem_limit_bytes=60 * MIB),
        cost_estimate=pl.CostEstimate(flops=4 * exp_local * picks * hidden * width, bytes_accessed=32 * MIB, transcendentals=0),
        name="weight_grads",
    )(ids, mix, hg, sq, x, g)


def combine_kernel(ids_ref, mix_ref, lat_ref, masks_ref, spread_ref, back_ref, lat_out, mix_out):
    picks, tokens = ids_ref.shape
    experts = spread_ref.shape[1]
    width = lat_ref.shape[1]
    half = width // 2
    main, low, high = (masks_ref[i] for i in range(3))
    front, tail = back_ref[:, :width], back_ref[:, width:]
    lat_out[:, :half] = (dot(main, front[:, :half]) + dot(low, tail)).astype(BF16)
    lat_out[:, half:] = (dot(main, front[:, half:]) + dot(high, tail)).astype(BF16)
    tail_dots = low.astype(F32) * dot(lat_ref[:, :half], tail, NT) + high.astype(F32) * dot(lat_ref[:, half:], tail, NT)
    gained = jnp.zeros((experts, tokens), F32)
    for i, dots in enumerate((main.astype(F32) * dot(lat_ref[...], front, NT), tail_dots)):
        upper = dots.astype(BF16)
        lower = (dots - upper.astype(F32)).astype(BF16)
        gained = gained + dot(spread_ref[i], upper, NT) + dot(spread_ref[i], lower, NT)
    e_at = iota((experts, tokens), 0)
    for k in range(picks):
        dots = jnp.sum(jnp.where(ids_ref[k : k + 1, :] == e_at, gained, 0.0), axis=0, keepdims=True)
        mix_out[k : k + 1, :] = dots / (2.0 * mix_ref[k : k + 1, :].astype(F32))


def combine_back(ids, mix, lat, masks, spread, back):
    return pl.pallas_call(
        combine_kernel,
        out_shape=[jax.ShapeDtypeStruct(lat.shape, BF16), jax.ShapeDtypeStruct(ids.shape, F32)],
        compiler_params=pltpu.CompilerParams(vmem_limit_bytes=32 * MIB),
        name="combine_back",
    )(ids, mix, lat, masks, spread, back)


def exchange(rows, owners):
    shape = rows.shape
    moved = lax.all_to_all(rows.reshape(owners, SUB, shape[1]), AXES, split_axis=0, concat_axis=0, tiled=True)
    return moved.reshape(shape)


def on_device(latent, grad_out, expert_ids, combine, w_up, w_down):
    owners = lax.axis_size("node") * lax.axis_size("local")
    experts = owners // 2 * w_up.shape[1]
    ids, mix = expert_ids.T, combine.T
    recv = exchange(pack(ids, mix, latent, grad_out, experts, owners), owners)
    x, g, hg, sq, back = expert_rows(recv, jnp.swapaxes(w_up, 2, 3), w_down)
    returned = exchange(back, owners)
    d_up, d_down, masks, spread = weight_grads(ids, mix, hg, sq, x, g, experts)
    lat_grad, mix_grad = combine_back(ids, mix, latent, masks, spread, returned)
    return lat_grad, mix_grad.T, jnp.swapaxes(d_up, 1, 2)[None], d_down[None]


def solution(mesh):
    in_specs = (
        P(AXES, None),
        P(AXES, None),
        P(AXES, None),
        P(AXES, None),
        P(AXES, None, None, None),
        P(AXES, None, None, None),
    )
    out_specs = (
        P(AXES, None),
        P(AXES, None),
        P(AXES, None, None, None),
        P(AXES, None, None, None),
    )
    return jax.shard_map(
        on_device, mesh=mesh, in_specs=in_specs, out_specs=out_specs, check_vma=False
    )
```

time: 303 us -> 169 us (0.56); the launches traced: 298 us -> 168 us
  waiting for transfers between devices: 114 us -> 24.3 us
  blocking collectives: 0 us -> 86.5 us
  local copies, waits for them, and re-layouts: 74.4 us -> 2.19 us
  matrix products: 50.5 us -> 0 us
  Pallas kernels: 0 us -> 49.9 us
  starting transfers between devices: 42.8 us -> 4.54 us
  other arithmetic: 15.6 us -> 0 us
    all_to_all x5 -> x1, waiting for transfers between devices: 114 us -> 24.3 us  [exchange(): lax.all_to_all(rows.reshape(owners, SUB, shape[1]), AXES, split_axis=0, c...]
    all_to_all x0 -> x1, blocking collectives: none -> 86.5 us  [exchange(): lax.all_to_all(rows.reshape(owners, SUB, shape[1]), AXES, split_axis=0, c...]
    dot_general x5 -> x0, matrix products: 50.5 us -> none  [the longest x1 13.2 us: batched_backward(): jnp.einsum('erl,ehl->erh', rows_grad, lower, preferred_element_type=jnp.f...]
    pallas_call x0 -> x4, Pallas kernels: none -> 49.9 us  [the longest x1 23.5 us: expert_rows(): pl.pallas_call(rows_kernel, in_specs=[IN_HBM] * 3, out_specs=[IN_HBM] * 5...]
    all_to_all x5 -> x1, starting transfers between devices: 42.8 us -> 4.54 us  [exchange(): lax.all_to_all(rows.reshape(owners, SUB, shape[1]), AXES, split_axis=0, c...]
    gather x7 -> x0, local copies, waits for them, and re-layouts: 30.5 us -> none  [the longest x1 9.46 us: fill_rows(): mix_rows.reshape(-1)[safe]]
    select_n x2 -> x0, local copies, waits for them, and re-layouts: 18.3 us -> none  [the longest x1 10.3 us: fill_rows(): jnp.where(valid[:, None], rows_grad[token_rows], jnp.zeros((), rows_grad....]
    reduce_sum x4 -> x0, other arithmetic: 9.96 us -> none  [the longest x1 7.52 us: on_device(): rows_back = back_in.reshape(exp_local, owner_count // 2, 2, cap_slots, la...]
  transfers between devices with their start and end apart: 5 -> 1, of which waited for: 3 -> 1; matrix products, arithmetic and copies ran while one was open for 29% -> 0% of each run, Pallas kernels for 0% -> 10%
where the time goes in v2:
time: 169 us; the launch traced here: 168 us
  blocking collectives  86.5 us (51%)
  Pallas kernels  49.9 us (30%)
  waiting for transfers between devices  24.3 us (14%)
  starting transfers between devices  4.54 us (3%)
  local copies, waits for them, and re-layouts  2.19 us (1%)
    all_to_all x1, blocking collectives, exchange(): lax.all_to_all(rows.reshape(owners, SUB, shape[1]), AXES, split_axis=0, c...  86.5 us
    all_to_all x1, waiting for transfers between devices, exchange(): lax.all_to_all(rows.reshape(owners, SUB, shape[1]), AXES, split_axis=0, c...  24.3 us
    pallas_call x1, Pallas kernels, expert_rows(): pl.pallas_call(rows_kernel, in_specs=[IN_HBM] * 3, out_specs=[IN_HBM] * 5...  23.5 us
    pallas_call x1, Pallas kernels, weight_grads(): pl.pallas_call(functools.partial(weights_kernel, experts), grid=(exp_loca...  16.7 us
    pallas_call x1, Pallas kernels, pack(): pl.pallas_call(pack_kernel, grid=(steps,), in_specs=[whole(ids), whole(mi...  6.33 us
    all_to_all x1, starting transfers between devices, exchange(): lax.all_to_all(rows.reshape(owners, SUB, shape[1]), AXES, split_axis=0, c...  4.54 us
  transfers between devices with their start and end apart: 1, of which 1 were waited for; matrix products, arithmetic and copies ran while one was open for 0% of the time, Pallas kernels for 10%

profile of v2, /device:TPU:1, one launch (start us, length us, event | category | flops | bytes accessed | tf_op | source)
XLA Modules:
  0.0 168.1 jit_solution(11898087337261015537)
XLA Ops:
  0.6 6.3 %pack.1 = bf16[1024,3072]{1,0:T(8,128)(2,1)} custom-call(s32[4,128]{1,0:T(4,128)} %bitcast.13, bf16[4,128]{1,0:T(4,128)(2,1)} %bitcast.16, bf16[128,1024]{1,0:T(8,128)(2,1)} %lat_ref.1, bf16[128,1024]{1,0:T(8,128)(2,1)} %grad_hbm.1), custom_call_target="tpu_custom_call" | custom-call | flops 1073741824 | bytes 6291456 | tf_op jit(solution)/shard_map/pack/pallas_call | solution.py:91
  7.0 86.5 %all_to_all.10 = bf16[128,8,3072]{2,1,0:T(8,128)(2,1)} all-to-all(bf16[128,8,3072]{2,1,0:T(8,128)(2,1)} %bitcast.19), channel_id=1, replica_groups=mesh['node'=8,'local'=16] {'node','local'}, dimensions={0} | all-to-all | bytes 12582912 | tf_op jit(solution)/shard_map/all_to_all | solution.py:312
  93.4 23.5 %expert_rows.1 = (bf16[2,768,1024]{2,1,0:T(8,128)(2,1)}, bf16[2,768,1024]{2,1,0:T(8,128)(2,1)}, bf16[2,1344,768]{2,1,0:T(8,128)(2,1)}, bf16[2,1344,768]{2,1,0:T(8,128)(2,1)}, bf16[1024,1536]{1,0:T(8,128)(2,1)}) custom-call(bf16[1024,3072]{1,0:T(8,128)(2,1)} %bitcast.20, bf16[1,2,1344,1024]{3,2,1,0:T(8,128)(2,1)} %bitcast.22, bf16[1,2,1344,1024]{3,2,1,0:T(8,128)(2,1)} %down_hbm.1), custom_call_target="tpu_custom_call" | custom-call | flops 12683575296 | bytes 33554432 | tf_op jit(solution)/shard_map/expert_rows/pallas_call | solution.py:225
  117.0 4.5 %all-to-all-start.1 = ((bf16[128,8,1536]{2,1,0:T(8,128)(2,1)}), bf16[128,8,1536]{2,1,0:T(8,128)(2,1)S(1)}, u32[]{:S(2)}, u32[]{:S(2)}) async-start(bf16[128,8,1536]{2,1,0:T(8,128)(2,1)} %bitcast.21), calls=%async_computation.1 | async-start | bytes 6291456 | tf_op jit(solution)/shard_map/all_to_all | solution.py:312
  121.5 0.0 copy-start
  121.5 0.0 copy-start.3
  121.5 0.0 copy-start.4
  121.6 16.7 %weight_grads.1 = (bf16[2,1344,1024]{2,1,0:T(8,128)(2,1)}, bf16[2,1344,1024]{2,1,0:T(8,128)(2,1)}, bf16[3,128,1024]{2,1,0:T(8,128)(2,1)}, bf16[2,128,1024]{2,1,0:T(8,128)(2,1)}) custom-call(s32[4,128]{1,0:T(4,128)} %bitcast.14, bf16[4,128]{1,0:T(4,128)(2,1)} %bitcast.17, bf16[2,1344,768]{2,1,0:T(8,128)(2,1)} %get-tuple-element.15.hg_ref, ...), custom_call_target="tpu_custom_call" | custom-call | flops 8455716864 | bytes 33554432 | tf_op jit(solution)/shard_map/weight_grads/pallas_call | solution.py:267
  138.3 24.3 %all-to-all-done.1 = bf16[128,8,1536]{2,1,0:T(8,128)(2,1)S(1)} async-done(((bf16[128,8,1536]{2,1,0:T(8,128)(2,1)}), bf16[128,8,1536]{2,1,0:T(8,128)(2,1)S(1)}, u32[]{:S(2)}, u32[]{:S(2)}) %all-to-all-start.1) | async-done | bytes 3145760 | tf_op jit(solution)/shard_map/all_to_all | solution.py:312
  162.6 0.0 copy-done
  162.6 0.0 copy-done.3
  162.6 0.0 copy-done.4
  162.6 0.0 copy-start.1
  162.6 1.1 copy-done.1
  163.7 0.0 copy-start.2
  163.7 1.0 copy-done.2
  164.8 3.4 %combine_back.1 = (bf16[128,1024]{1,0:T(8,128)(2,1)}, f32[4,128]{1,0:T(4,128)}) custom-call(s32[4,128]{1,0:T(4,128)S(1)} %bitcast.15, bf16[4,128]{1,0:T(4,128)(2,1)S(1)} %bitcast.18, bf16[128,1024]{1,0:T(8,128)(2,1)S(1)} %copy-done, bf16[3,128,1024]{2,1,0:T(8,128)(2,1)S(1)} %copy-done.1, bf16[2,128,1024]{2,1,0:T(8,128)(2,1)S(1)} %copy-done.2, ...), custom_call_target="tpu_custom_call" | custom-call | tf_op jit(solution)/shard_map/combine_back/pallas_call | solution.py:302
Async XLA Ops:
  117.0 45.6 %all-to-all-start.1 = ((bf16[128,8,1536]{2,1,0:T(8,128)(2,1)}), bf16[128,8,1536]{2,1,0:T(8,128)(2,1)S(1)}, u32[]{:S(2)}, u32[]{:S(2)}) async-start(bf16[128,8,1536]{2,1,0:T(8,128)(2,1)} %bitcast.21), calls=%async_computation.1 | async-start | bytes 6291456 | tf_op jit(solution)/shard_map/all_to_all | solution.py:312
  121.5 41.0 %copy-start = (bf16[128,1024]{1,0:T(8,128)(2,1)S(1)}, bf16[128,1024]{1,0:T(8,128)(2,1)}, u32[]{:S(2)}) copy-start(bf16[128,1024]{1,0:T(8,128)(2,1)} %lat_ref.1) | copy-start | bytes 786436
  121.5 41.0 %copy-start.3 = (s32[128,4]{0,1:T(4,128)S(1)}, s32[128,4]{0,1:T(4,128)}, u32[]{:S(2)}) copy-start(s32[128,4]{0,1:T(4,128)} %param.8) | copy-start | bytes 6148
  121.5 41.0 %copy-start.4 = (bf16[128,4]{0,1:T(4,128)(2,1)S(1)}, bf16[128,4]{0,1:T(4,128)(2,1)}, u32[]{:S(2)}) copy-start(bf16[128,4]{0,1:T(4,128)(2,1)} %param.9) | copy-start | bytes 3076
  162.6 1.1 copy-start.1
  163.7 1.0 copy-start.2

commit v3 on v2

--- a/solution.py
+++ b/solution.py
@@ -18,6 +18,7 @@
 TN = (((0,), (0,)), ((), ()))
 AXES = ("node", "local")
 IN_HBM = pl.BlockSpec(memory_space=pltpu.HBM)
+IN_VMEM = pl.BlockSpec(memory_space=pltpu.VMEM)
 
 
 def dot(a, b, dims=NN):
@@ -26,6 +27,10 @@
 
 def iota(shape, dim):
     return lax.broadcasted_iota(jnp.int32, shape, dim)
+
+
+def pinned(a):
+    return pltpu.with_memory_space_constraint(a, pltpu.HBM)
 
 
 def one_hot(mask):
@@ -69,24 +74,30 @@
         one.wait()
         two.wait()
 
-    at = (iota((rows, experts), 0) + step * rows) >> 4
-    e_at = iota((rows, experts), 1)
+    half = rows // 2
+    at = (iota((half, experts), 0) + step * half) >> 3
+    e_at = iota((half, experts), 1)
     even, odd = one_hot(e_at == 2 * at), one_hot(e_at == 2 * at + 1)
-    s = iota((rows, tokens), 0) & 7
+    s = iota((half, tokens), 0) & 7
     code0 = dot(even, code_s[...]).astype(jnp.int32)
     code1 = dot(odd, code_s[...]).astype(jnp.int32)
     weight0, weight1 = dot(even, weight_s[...]), dot(odd, weight_s[...])
     main, low, high = slot_masks(code0, code1, s)
-    out_ref[:, :width] = dot(one_hot(main), both_s[:tokens, :]).astype(BF16)
+
+    def twice(a):
+        a = a.reshape(half // SUB, 1, SUB, width)
+        return jnp.broadcast_to(a, (half // SUB, 2, SUB, width)).reshape(rows, width).astype(BF16)
+
+    out_ref[:, :width] = twice(dot(one_hot(main), both_s[:tokens, :]))
     mixed = jnp.where(main, jnp.where(s < CAP, weight0, weight1), 0.0).astype(BF16)
-    out_ref[:, width : 2 * width] = dot(mixed, both_s[tokens:, :]).astype(BF16)
+    out_ref[:, width : 2 * width] = twice(dot(mixed, both_s[tokens:, :]))
     rest = jnp.concatenate([jnp.where(low, 1.0, 0.0), jnp.where(high, weight1, 0.0)], axis=1)
-    out_ref[:, 2 * width :] = dot(rest.astype(BF16), both_s[...]).astype(BF16)
+    out_ref[:, 2 * width :] = twice(dot(rest.astype(BF16), both_s[...]))
 
 
 def pack(ids, mix, lat, grad, experts, owners):
     tokens, width = lat.shape
-    rows, steps = owners * SUB, 4
+    rows, steps = owners * SUB, 2
     whole = lambda a: pl.BlockSpec(a.shape, lambda i: (0, 0))
     return pl.pallas_call(
         pack_kernel,
@@ -117,12 +128,12 @@
 
 
 def rows_kernel(
-    recv_hbm, up_hbm, down_hbm, x_hbm, g_hbm, hg_hbm, sq_hbm, back_hbm,
-    recv_s, up_s, down_s, x_s, g_s, hg_s, sq_s, y_s, back_s, recv_sems, sems, back_sems,
+    recv_ref, up_ref, down_ref, x_hbm, g_hbm, hg_hbm, sq_hbm, back_hbm,
+    x_s, g_s, hg_s, sq_s, y_s, back_s, sems, back_sems,
 ):
-    exp_local, hidden, width = up_s.shape
+    exp_local, hidden, width = up_ref.shape[1:]
     half, quarter = width // 2, GROUP // 2
-    groups = recv_s.shape[0] // GROUP
+    groups = recv_ref.shape[0] // GROUP
     picks = x_s.shape[1]
     first = GROUP // SUB * CAP
     second = GROUP - first
@@ -133,34 +144,17 @@
         scratch, hbm = kept[which]
         return pltpu.make_async_copy(scratch.at[j], hbm.at[j], sems.at[which, j])
 
-    def load_rows(i):
-        raw = pl.ds(pl.multiple_of(i * GROUP, GROUP), GROUP)
-        return pltpu.make_async_copy(recv_hbm.at[raw], recv_s.at[raw], recv_sems.at[i])
-
-    def load_up(j):
-        return pltpu.make_async_copy(up_hbm.at[0, j], up_s.at[j], sems.at[4, j])
-
-    def load_down(j):
-        return pltpu.make_async_copy(down_hbm.at[0, j], down_s.at[j], sems.at[5, j])
-
-    for i in range(groups):
-        load_rows(i).start()
-    for j in range(exp_local):
-        load_up(j).start()
-        load_down(j).start()
-
     take, take_tail = slot_order(square, 0, False), slot_order(square, 0, True)
 
     def unfold(i, carry):
-        load_rows(i).wait()
         raw = pl.ds(pl.multiple_of(i * GROUP, GROUP), GROUP)
         at = pl.multiple_of(i * first, second)
         whole, head, tail = pl.ds(at, first), pl.ds(at, second), pl.ds(at + second, quarter)
         for to, cols in ((x_s, slice(0, width)), (g_s, slice(width, 2 * width))):
-            moved = dot(take, recv_s[raw, cols]).astype(BF16)
+            moved = dot(take, recv_ref[raw, cols]).astype(BF16)
             to[0, whole, :] = moved[:first]
             to[1, head, :] = moved[first:]
-        moved = dot(take_tail, recv_s[raw, 2 * width :]).astype(BF16)
+        moved = dot(take_tail, recv_ref[raw, 2 * width :]).astype(BF16)
         x_s[1, tail, :] = moved[:quarter]
         g_s[1, tail, :] = moved[quarter:]
         return carry
@@ -170,26 +164,23 @@
         keep(0, j).start()
         keep(1, j).start()
 
-    block, tile = hidden // 3, 256
+    blocks = 1
+    block = hidden // blocks
     for j in range(exp_local):
-        load_up(j).wait()
-        load_down(j).wait()
 
         def forward(i, carry):
             at = pl.ds(pl.multiple_of(i * block, 64), block)
-            pre = dot(up_s[j, at, :], x_s[j], NT)
-            pulled = dot(down_s[j, at, :], g_s[j], NT)
+            pre = dot(up_ref[0, j, at, :], x_s[j], NT)
+            pulled = dot(down_ref[0, j, at, :], g_s[j], NT)
             act = jnp.maximum(pre, 0.0)
             sq_s[j, at, :] = (act * act).astype(BF16)
             hg_s[j, at, :] = (2.0 * act * pulled).astype(BF16)
             return carry
 
-        lax.fori_loop(0, 3, forward, 0)
+        lax.fori_loop(0, blocks, forward, 0)
         keep(2, j).start()
         keep(3, j).start()
-        for c in range(picks // tile):
-            cols = slice(c * tile, (c + 1) * tile)
-            y_s[j, cols, :] = dot(hg_s[j, :, cols], up_s[j], TN).astype(BF16)
+        y_s[j] = dot(hg_s[j], up_ref[0, j], TN).astype(BF16)
 
     put, put_tail = slot_order(square, 1, False), slot_order(square, 1, True)
 
@@ -224,12 +215,12 @@
     back = (rows, 3 * width // 2)
     return pl.pallas_call(
         rows_kernel,
-        in_specs=[IN_HBM] * 3,
+        in_specs=[IN_VMEM] * 3,
         out_specs=[IN_HBM] * 5,
         out_shape=[pltpu.HBM(shape, BF16) for shape in kept + [back]],
-        scratch_shapes=[pltpu.VMEM(shape, BF16) for shape in [recv.shape, up.shape[1:], up.shape[1:]] + kept + [kept[0], back]]
-        + [pltpu.SemaphoreType.DMA(n) for n in ((rows // GROUP,), (6, exp_local), (rows // GROUP,))],
-        compiler_params=pltpu.CompilerParams(vmem_limit_bytes=56 * MIB),
+        scratch_shapes=[pltpu.VMEM(shape, BF16) for shape in kept + [kept[0], back]]
+        + [pltpu.SemaphoreType.DMA(n) for n in ((4, exp_local), (rows // GROUP,))],
+        compiler_params=pltpu.CompilerParams(vmem_limit_bytes=36 * MIB),
         cost_estimate=pl.CostEstimate(flops=6 * exp_local * picks * hidden * width, bytes_accessed=32 * MIB, transcendentals=0),
         name="expert_rows",
     )(recv, up, down)
@@ -304,7 +295,7 @@
         out_shape=[jax.ShapeDtypeStruct(lat.shape, BF16), jax.ShapeDtypeStruct(ids.shape, F32)],
         compiler_params=pltpu.CompilerParams(vmem_limit_bytes=32 * MIB),
         name="combine_back",
-    )(ids, mix, lat, masks, spread, back)
+    )(ids, mix, lat, pinned(masks), pinned(spread), back)
 
 
 def exchange(rows, owners):

time: 169 us -> 162 us (0.959)
  Pallas kernels: 49.9 us -> 45.5 us
  local copies, waits for them, and re-layouts: 2.19 us -> 0.04 us
    pallas_call x1, Pallas kernels: 23.5 us -> 18.9 us  [expert_rows(): pl.pallas_call(rows_kernel, in_specs=[IN_VMEM] * 3, out_specs=[IN_HBM] *...]
    unnamed x10 -> x12, local copies, waits for them, and re-layouts: 2.19 us -> 0.04 us
where the time goes in v3:
time: 162 us; the launch traced here: 161 us
  blocking collectives  86.4 us (53%)
  Pallas kernels  45.5 us (28%)
  waiting for transfers between devices  24.3 us (15%)
  starting transfers between devices  4.52 us (3%)
    all_to_all x1, blocking collectives, exchange(): lax.all_to_all(rows.reshape(owners, SUB, shape[1]), AXES, split_axis=0, c...  86.4 us
    all_to_all x1, waiting for transfers between devices, exchange(): lax.all_to_all(rows.reshape(owners, SUB, shape[1]), AXES, split_axis=0, c...  24.3 us
    pallas_call x1, Pallas kernels, expert_rows(): pl.pallas_call(rows_kernel, in_specs=[IN_VMEM] * 3, out_specs=[IN_HBM] *...  18.9 us
    pallas_call x1, Pallas kernels, weight_grads(): pl.pallas_call(functools.partial(weights_kernel, experts), grid=(exp_loca...  16.7 us
    pallas_call x1, Pallas kernels, pack(): pl.pallas_call(pack_kernel, grid=(steps,), in_specs=[whole(ids), whole(mi...  5.23 us
    pallas_call x1, Pallas kernels, combine_back(): pl.pallas_call(combine_kernel, out_shape=[jax.ShapeDtypeStruct(lat.shape,...  4.65 us
    all_to_all x1, starting transfers between devices, exchange(): lax.all_to_all(rows.reshape(owners, SUB, shape[1]), AXES, split_axis=0, c...  4.52 us
  transfers between devices with their start and end apart: 1, of which 1 were waited for; matrix products, arithmetic and copies ran while one was open for 0% of the time, Pallas kernels for 10%

profile of v3, /device:TPU:1, one launch (start us, length us, event | category | flops | bytes accessed | tf_op | source)
XLA Modules:
  0.0 161.5 jit_solution(4574378991914509914)
XLA Ops:
  0.6 0.0 slice-start
  0.6 5.2 %pack.1 = bf16[1024,3072]{1,0:T(8,128)(2,1)} custom-call(s32[4,128]{1,0:T(4,128)} %bitcast.14, bf16[4,128]{1,0:T(4,128)(2,1)} %bitcast.17, bf16[128,1024]{1,0:T(8,128)(2,1)} %lat_ref.1, bf16[128,1024]{1,0:T(8,128)(2,1)} %grad_hbm.1), custom_call_target="tpu_custom_call" | custom-call | flops 1073741824 | bytes 6291456 | tf_op jit(solution)/shard_map/pack/pallas_call | solution.py:102
  5.9 0.0 slice-start.1
  5.9 0.0 copy-start.3
  5.9 86.4 %all_to_all.10 = bf16[128,8,3072]{2,1,0:T(8,128)(2,1)S(1)} all-to-all(bf16[128,8,3072]{2,1,0:T(8,128)(2,1)} %bitcast.23), channel_id=1, replica_groups=mesh['node'=8,'local'=16] {'node','local'}, dimensions={0} | all-to-all | bytes 12582912 | tf_op jit(solution)/shard_map/all_to_all | solution.py:303
  92.3 0.0 slice-done
  92.3 0.0 slice-done.1
  92.3 0.0 copy-done.3
  92.3 18.9 %expert_rows.1 = (bf16[2,768,1024]{2,1,0:T(8,128)(2,1)}, bf16[2,768,1024]{2,1,0:T(8,128)(2,1)}, bf16[2,1344,768]{2,1,0:T(8,128)(2,1)}, bf16[2,1344,768]{2,1,0:T(8,128)(2,1)}, bf16[1024,1536]{1,0:T(8,128)(2,1)}) custom-call(bf16[1024,3072]{1,0:T(8,128)(2,1)S(1)} %bitcast.13, bf16[1,2,1344,1024]{3,2,1,0:T(8,128)(2,1)S(1)} %bitcast.22, ...), custom_call_target="tpu_custom_call" | custom-call | flops 12683575296 | bytes 33554432 | tf_op jit(solution)/shard_map/expert_rows/pallas_call | solution.py:216
  111.2 4.5 %all-to-all-start.1 = ((bf16[128,8,1536]{2,1,0:T(8,128)(2,1)}), bf16[128,8,1536]{2,1,0:T(8,128)(2,1)S(1)}, u32[]{:S(2)}, u32[]{:S(2)}) async-start(bf16[128,8,1536]{2,1,0:T(8,128)(2,1)} %bitcast.24), calls=%async_computation.1 | async-start | bytes 6291456 | tf_op jit(solution)/shard_map/all_to_all | solution.py:303
  115.8 0.0 copy-start
  115.8 0.0 copy-start.1
  115.8 0.0 copy-start.2
  115.8 16.7 %weight_grads.1 = (bf16[2,1344,1024]{2,1,0:T(8,128)(2,1)}, bf16[2,1344,1024]{2,1,0:T(8,128)(2,1)}, bf16[3,128,1024]{2,1,0:T(8,128)(2,1)}, bf16[2,128,1024]{2,1,0:T(8,128)(2,1)}) custom-call(s32[4,128]{1,0:T(4,128)} %bitcast.15, bf16[4,128]{1,0:T(4,128)(2,1)} %bitcast.18, bf16[2,1344,768]{2,1,0:T(8,128)(2,1)} %get-tuple-element.15.hg_ref, ...), custom_call_target="tpu_custom_call" | custom-call | flops 8455716864 | bytes 33554432 | tf_op jit(solution)/shard_map/weight_grads/pallas_call | solution.py:258
  132.5 24.3 %all-to-all-done.1 = bf16[128,8,1536]{2,1,0:T(8,128)(2,1)S(1)} async-done(((bf16[128,8,1536]{2,1,0:T(8,128)(2,1)}), bf16[128,8,1536]{2,1,0:T(8,128)(2,1)S(1)}, u32[]{:S(2)}, u32[]{:S(2)}) %all-to-all-start.1) | async-done | bytes 3145760 | tf_op jit(solution)/shard_map/all_to_all | solution.py:303
  156.8 0.0 copy-done
  156.8 0.0 copy-done.1
  156.8 0.0 copy-done.2
  156.8 4.7 %combine_back.1 = (bf16[128,1024]{1,0:T(8,128)(2,1)}, f32[4,128]{1,0:T(4,128)}) custom-call(s32[4,128]{1,0:T(4,128)S(1)} %bitcast.16, bf16[4,128]{1,0:T(4,128)(2,1)S(1)} %bitcast.19, bf16[128,1024]{1,0:T(8,128)(2,1)S(1)} %copy-done, bf16[3,128,1024]{2,1,0:T(8,128)(2,1)} %get-tuple-element.19.masks_ref, bf16[2,128,1024]{2,1,0:T(8,128)(2,1)} %get-tuple-element.20.spread_ref, ...), custom_call_target="tpu_custom_call" | custom-call | tf_op jit(solution)/shard_map/combine_back/pallas_call | solution.py:293
  (1 shorter events, 0.0 us)
Async XLA Ops:
  0.6 91.7 %slice-start = ((s8[5505024]{0:T(1024)(128)(4,1)}), s8[1310720]{0:T(1024)(128)(4,1)S(1)}, s32[]{:S(2)}) async-start(s8[5505024]{0:T(1024)(128)(4,1)} %bitcast.20), calls=%async_computation.2 | async-start | bytes 2621440
  5.9 86.4 %slice-start.1 = ((s8[5505024]{0:T(1024)(128)(4,1)}), s8[4194304]{0:T(1024)(128)(4,1)S(1)}, s32[]{:S(2)}) async-start(s8[5505024]{0:T(1024)(128)(4,1)} %bitcast.20), calls=%async_computation.3 | async-start | bytes 8388608
  5.9 86.4 %copy-start.3 = (bf16[1,2,1344,1024]{3,2,1,0:T(8,128)(2,1)S(1)}, bf16[1,2,1344,1024]{3,2,1,0:T(8,128)(2,1)}, u32[]{:S(2)}) copy-start(bf16[1,2,1344,1024]{3,2,1,0:T(8,128)(2,1)} %down_ref.1) | copy-start | bytes 16515076
  111.2 45.6 %all-to-all-start.1 = ((bf16[128,8,1536]{2,1,0:T(8,128)(2,1)}), bf16[128,8,1536]{2,1,0:T(8,128)(2,1)S(1)}, u32[]{:S(2)}, u32[]{:S(2)}) async-start(bf16[128,8,1536]{2,1,0:T(8,128)(2,1)} %bitcast.24), calls=%async_computation.1 | async-start | bytes 6291456 | tf_op jit(solution)/shard_map/all_to_all | solution.py:303
  115.8 41.1 %copy-start = (bf16[128,1024]{1,0:T(8,128)(2,1)S(1)}, bf16[128,1024]{1,0:T(8,128)(2,1)}, u32[]{:S(2)}) copy-start(bf16[128,1024]{1,0:T(8,128)(2,1)} %lat_ref.1) | copy-start | bytes 786436
  115.8 41.0 %copy-start.1 = (s32[128,4]{0,1:T(4,128)S(1)}, s32[128,4]{0,1:T(4,128)}, u32[]{:S(2)}) copy-start(s32[128,4]{0,1:T(4,128)} %param.8) | copy-start | bytes 6148
  115.8 41.0 %copy-start.2 = (bf16[128,4]{0,1:T(4,128)(2,1)S(1)}, bf16[128,4]{0,1:T(4,128)(2,1)}, u32[]{:S(2)}) copy-start(bf16[128,4]{0,1:T(4,128)(2,1)} %param.9) | copy-start | bytes 3076

commit v4 on v3

--- a/solution.py
+++ b/solution.py
@@ -57,64 +57,68 @@
     return main, (s < 4) & (code1 == s + 3), (s >= 4) & (code1 == s - 1)
 
 
-def pack_kernel(ids_ref, mix_ref, lat_hbm, grad_hbm, out_ref, code_s, weight_s, both_s, sems):
-    step = pl.program_id(0)
-    experts, tokens = code_s.shape
-    rows, width = out_ref.shape[0], lat_hbm.shape[1]
-
-    @pl.when(step == 0)
-    def _():
-        one = pltpu.make_async_copy(lat_hbm, both_s.at[pl.ds(0, tokens)], sems.at[0])
-        two = pltpu.make_async_copy(grad_hbm, both_s.at[pl.ds(tokens, tokens)], sems.at[1])
-        one.start()
-        two.start()
-        code, weight = pick_codes(ids_ref[...], mix_ref[...].astype(F32), experts)
-        code_s[...] = code
-        weight_s[...] = weight
-        one.wait()
-        two.wait()
-
-    half = rows // 2
-    at = (iota((half, experts), 0) + step * half) >> 3
+def pack_kernel(ids_hbm, mix_hbm, lat_hbm, grad_hbm, out_ref, ids_s, mix_s, both_s, sems):
+    tokens, width = lat_hbm.shape
+    rows, experts = out_ref.shape[0], out_ref.shape[0] // SUB
+    half, part = rows // 2, rows // 4
+    loads = [
+        pltpu.make_async_copy(hbm, to, sems.at[i])
+        for i, (hbm, to) in enumerate(
+            (
+                (ids_hbm, ids_s),
+                (mix_hbm, mix_s),
+                (lat_hbm, both_s.at[pl.ds(0, tokens)]),
+                (grad_hbm, both_s.at[pl.ds(tokens, tokens)]),
+            )
+        )
+    ]
+    for load in loads:
+        load.start()
+    at = iota((half, experts), 0) >> 3
     e_at = iota((half, experts), 1)
     even, odd = one_hot(e_at == 2 * at), one_hot(e_at == 2 * at + 1)
     s = iota((half, tokens), 0) & 7
-    code0 = dot(even, code_s[...]).astype(jnp.int32)
-    code1 = dot(odd, code_s[...]).astype(jnp.int32)
-    weight0, weight1 = dot(even, weight_s[...]), dot(odd, weight_s[...])
+    loads[0].wait()
+    loads[1].wait()
+    code, weight = pick_codes(ids_s[...], mix_s[...].astype(F32), experts)
+    code0, code1 = dot(even, code).astype(jnp.int32), dot(odd, code).astype(jnp.int32)
+    weight0, weight1 = dot(even, weight), dot(odd, weight)
     main, low, high = slot_masks(code0, code1, s)
+    plain = one_hot(main)
+    mixed = jnp.where(main, jnp.where(s < CAP, weight0, weight1), 0.0).astype(BF16)
+    rest = jnp.concatenate([jnp.where(low, 1.0, 0.0), jnp.where(high, weight1, 0.0)], axis=1).astype(BF16)
+    loads[2].wait()
+    loads[3].wait()
 
     def twice(a):
-        a = a.reshape(half // SUB, 1, SUB, width)
-        return jnp.broadcast_to(a, (half // SUB, 2, SUB, width)).reshape(rows, width).astype(BF16)
-
-    out_ref[:, :width] = twice(dot(one_hot(main), both_s[:tokens, :]))
-    mixed = jnp.where(main, jnp.where(s < CAP, weight0, weight1), 0.0).astype(BF16)
-    out_ref[:, width : 2 * width] = twice(dot(mixed, both_s[tokens:, :]))
-    rest = jnp.concatenate([jnp.where(low, 1.0, 0.0), jnp.where(high, weight1, 0.0)], axis=1)
-    out_ref[:, 2 * width :] = twice(dot(rest.astype(BF16), both_s[...]))
-
-
-def pack(ids, mix, lat, grad, experts, owners):
+        a = a.reshape(part // SUB, 1, SUB, width)
+        return jnp.broadcast_to(a, (part // SUB, 2, SUB, width)).reshape(2 * part, width).astype(BF16)
+
+    for i in range(2):
+        here, to = slice(i * part, (i + 1) * part), slice(i * 2 * part, (i + 1) * 2 * part)
+        out_ref[to, :width] = twice(dot(plain[here], both_s[:tokens, :]))
+        out_ref[to, width : 2 * width] = twice(dot(mixed[here], both_s[tokens:, :]))
+        out_ref[to, 2 * width :] = twice(dot(rest[here], both_s[...]))
+
+
+def pack(ids, mix, lat, grad, owners):
     tokens, width = lat.shape
-    rows, steps = owners * SUB, 2
-    whole = lambda a: pl.BlockSpec(a.shape, lambda i: (0, 0))
+    rows = owners * SUB
     return pl.pallas_call(
         pack_kernel,
-        grid=(steps,),
-        in_specs=[whole(ids), whole(mix), IN_HBM, IN_HBM],
-        out_specs=pl.BlockSpec((rows // steps, 3 * width), lambda i: (i, 0)),
+        in_specs=[IN_HBM] * 4,
+        out_specs=IN_VMEM,
         out_shape=jax.ShapeDtypeStruct((rows, 3 * width), BF16),
         scratch_shapes=[
-            pltpu.VMEM((experts, tokens), BF16),
-            pltpu.VMEM((experts, tokens), BF16),
+            pltpu.VMEM(ids.shape, jnp.int32),
+            pltpu.VMEM(mix.shape, BF16),
             pltpu.VMEM((2 * tokens, width), BF16),
-            pltpu.SemaphoreType.DMA((2,)),
+            pltpu.SemaphoreType.DMA((4,)),
         ],
-        compiler_params=pltpu.CompilerParams(vmem_limit_bytes=60 * MIB),
+        compiler_params=pltpu.CompilerParams(vmem_limit_bytes=24 * MIB),
         cost_estimate=pl.CostEstimate(flops=8 * rows * tokens * width, bytes_accessed=6 * rows * width, transcendentals=0),
         name="pack",
-    )(ids, mix, lat, grad)
+    )(pinned(ids), pinned(mix), pinned(lat), pinned(grad))
 
 
 def slot_order(shape, pick_dim, tail):
@@ -268,21 +272,29 @@
     )(ids, mix, hg, sq, x, g)
 
 
-def combine_kernel(ids_ref, mix_ref, lat_ref, masks_ref, spread_ref, back_ref, lat_out, mix_out):
+def combine_kernel(ids_ref, mix_ref, lat_ref, masks_hbm, spread_hbm, back_ref, lat_out, mix_out, masks_s, spread_s, sems):
     picks, tokens = ids_ref.shape
-    experts = spread_ref.shape[1]
+    experts = spread_s.shape[1]
     width = lat_ref.shape[1]
     half = width // 2
-    main, low, high = (masks_ref[i] for i in range(3))
-    front, tail = back_ref[:, :width], back_ref[:, width:]
-    lat_out[:, :half] = (dot(main, front[:, :half]) + dot(low, tail)).astype(BF16)
-    lat_out[:, half:] = (dot(main, front[:, half:]) + dot(high, tail)).astype(BF16)
-    tail_dots = low.astype(F32) * dot(lat_ref[:, :half], tail, NT) + high.astype(F32) * dot(lat_ref[:, half:], tail, NT)
+    load_masks = pltpu.make_async_copy(masks_hbm, masks_s, sems.at[0])
+    load_spread = pltpu.make_async_copy(spread_hbm, spread_s, sems.at[1])
+    load_masks.start()
+    load_spread.start()
+    front_dots = dot(lat_ref[...], back_ref[:, :width], NT)
+    low_dots = dot(lat_ref[:, :half], back_ref[:, width:], NT)
+    high_dots = dot(lat_ref[:, half:], back_ref[:, width:], NT)
+    load_masks.wait()
+    main, low, high = (masks_s[i] for i in range(3))
+    tail = back_ref[:, width:]
+    lat_out[:, :half] = (dot(main, back_ref[:, :half]) + dot(low, tail)).astype(BF16)
+    lat_out[:, half:] = (dot(main, back_ref[:, half:width]) + dot(high, tail)).astype(BF16)
+    load_spread.wait()
     gained = jnp.zeros((experts, tokens), F32)
-    for i, dots in enumerate((main.astype(F32) * dot(lat_ref[...], front, NT), tail_dots)):
+    for i, dots in enumerate((main.astype(F32) * front_dots, low.astype(F32) * low_dots + high.astype(F32) * high_dots)):
         upper = dots.astype(BF16)
         lower = (dots - upper.astype(F32)).astype(BF16)
-        gained = gained + dot(spread_ref[i], upper, NT) + dot(spread_ref[i], lower, NT)
+        gained = gained + dot(spread_s[i], upper, NT) + dot(spread_s[i], lower, NT)
     e_at = iota((experts, tokens), 0)
     for k in range(picks):
         dots = jnp.sum(jnp.where(ids_ref[k : k + 1, :] == e_at, gained, 0.0), axis=0, keepdims=True)
@@ -292,7 +304,10 @@
 def combine_back(ids, mix, lat, masks, spread, back):
     return pl.pallas_call(
         combine_kernel,
+        in_specs=[IN_VMEM] * 3 + [IN_HBM] * 2 + [IN_VMEM],
+        out_specs=[IN_VMEM] * 2,
         out_shape=[jax.ShapeDtypeStruct(lat.shape, BF16), jax.ShapeDtypeStruct(ids.shape, F32)],
+        scratch_shapes=[pltpu.VMEM(masks.shape, BF16), pltpu.VMEM(spread.shape, BF16), pltpu.SemaphoreType.DMA((2,))],
         compiler_params=pltpu.CompilerParams(vmem_limit_bytes=32 * MIB),
         name="combine_back",
     )(ids, mix, lat, pinned(masks), pinned(spread), back)
@@ -308,7 +323,7 @@
     owners = lax.axis_size("node") * lax.axis_size("local")
     experts = owners // 2 * w_up.shape[1]
     ids, mix = expert_ids.T, combine.T
-    recv = exchange(pack(ids, mix, latent, grad_out, experts, owners), owners)
+    recv = exchange(pack(ids, mix, latent, grad_out, owners), owners)
     x, g, hg, sq, back = expert_rows(recv, jnp.swapaxes(w_up, 2, 3), w_down)
     returned = exchange(back, owners)
     d_up, d_down, masks, spread = weight_grads(ids, mix, hg, sq, x, g, experts)

time: 162 us -> 158 us (0.975)
  Pallas kernels: 45.5 us -> 41.7 us
    pallas_call x2, Pallas kernels: 9.88 us -> 6.06 us  [the longest x1 3.69 us: combine_back(): pl.pallas_call(combine_kernel, in_specs=[IN_VMEM] * 3 + [IN_HBM] * 2 + [I...]
  transfers between devices with their start and end apart: 1 -> 1, of which waited for: 1 -> 1; matrix products, arithmetic and copies ran while one was open for 0% -> 0% of each run, Pallas kernels for 10% -> 11%
where the time goes in v4:
time: 158 us
  blocking collectives  86.2 us (55%)
  Pallas kernels  41.7 us (26%)
  waiting for transfers between devices  24.3 us (15%)
  starting transfers between devices  4.53 us (3%)
    all_to_all x1, blocking collectives, exchange(): lax.all_to_all(rows.reshape(owners, SUB, shape[1]), AXES, split_axis=0, c...  86.2 us
    all_to_all x1, waiting for transfers between devices, exchange(): lax.all_to_all(rows.reshape(owners, SUB, shape[1]), AXES, split_axis=0, c...  24.3 us
    pallas_call x1, Pallas kernels, expert_rows(): pl.pallas_call(rows_kernel, in_specs=[IN_VMEM] * 3, out_specs=[IN_HBM] *...  18.9 us
    pallas_call x1, Pallas kernels, weight_grads(): pl.pallas_call(functools.partial(weights_kernel, experts), grid=(exp_loca...  16.7 us
    all_to_all x1, starting transfers between devices, exchange(): lax.all_to_all(rows.reshape(owners, SUB, shape[1]), AXES, split_axis=0, c...  4.53 us
    pallas_call x1, Pallas kernels, combine_back(): pl.pallas_call(combine_kernel, in_specs=[IN_VMEM] * 3 + [IN_HBM] * 2 + [I...  3.69 us
  transfers between devices with their start and end apart: 1, of which 1 were waited for; matrix products, arithmetic and copies ran while one was open for 0% of the time, Pallas kernels for 11%

profile of v4, /device:TPU:1, one launch (start us, length us, event | category | flops | bytes accessed | tf_op | source)
XLA Modules:
  0.0 157.6 jit_solution(2045322571577554114)
XLA Ops:
  0.6 0.0 slice-start
  0.6 0.0 slice-start.2
  0.7 2.4 %pack.1 = bf16[1024,3072]{1,0:T(8,128)(2,1)S(1)} custom-call(s32[4,128]{1,0:T(4,128)} %bitcast.15, bf16[4,128]{1,0:T(4,128)(2,1)} %bitcast.18, bf16[128,1024]{1,0:T(8,128)(2,1)} %lat_ref.1, bf16[128,1024]{1,0:T(8,128)(2,1)} %grad_hbm.1), custom_call_target="tpu_custom_call" | custom-call | flops 1073741824 | bytes 6291456 | tf_op jit(solution)/shard_map/pack/pallas_call | solution.py:107
  3.0 0.0 slice-start.1
  3.0 0.0 slice-start.3
  3.1 86.2 %all_to_all.10 = bf16[128,8,3072]{2,1,0:T(8,128)(2,1)S(1)} all-to-all(bf16[128,8,3072]{2,1,0:T(8,128)(2,1)S(1)} %bitcast.12), channel_id=1, replica_groups=mesh['node'=8,'local'=16] {'node','local'}, dimensions={0} | all-to-all | bytes 12582912 | tf_op jit(solution)/shard_map/all_to_all | solution.py:318
  89.2 0.0 slice-done
  89.2 0.0 slice-done.2
  89.2 0.0 slice-done.1
  89.2 0.0 slice-done.3
  89.3 18.9 %expert_rows.1 = (bf16[2,768,1024]{2,1,0:T(8,128)(2,1)}, bf16[2,768,1024]{2,1,0:T(8,128)(2,1)}, bf16[2,1344,768]{2,1,0:T(8,128)(2,1)}, bf16[2,1344,768]{2,1,0:T(8,128)(2,1)}, bf16[1024,1536]{1,0:T(8,128)(2,1)}) custom-call(bf16[1024,3072]{1,0:T(8,128)(2,1)S(1)} %bitcast.14, bf16[1,2,1344,1024]{3,2,1,0:T(8,128)(2,1)S(1)} %bitcast.23, ...), custom_call_target="tpu_custom_call" | custom-call | flops 12683575296 | bytes 33554432 | tf_op jit(solution)/shard_map/expert_rows/pallas_call | solution.py:220
  108.2 4.5 %all-to-all-start.1 = ((bf16[128,8,1536]{2,1,0:T(8,128)(2,1)}), bf16[128,8,1536]{2,1,0:T(8,128)(2,1)S(1)}, u32[]{:S(2)}, u32[]{:S(2)}) async-start(bf16[128,8,1536]{2,1,0:T(8,128)(2,1)} %bitcast.26), calls=%async_computation.1 | async-start | bytes 6291456 | tf_op jit(solution)/shard_map/all_to_all | solution.py:318
  112.7 0.0 copy-start
  112.7 0.0 copy-start.1
  112.8 0.0 copy-start.2
  112.8 16.7 %weight_grads.1 = (bf16[2,1344,1024]{2,1,0:T(8,128)(2,1)}, bf16[2,1344,1024]{2,1,0:T(8,128)(2,1)}, bf16[3,128,1024]{2,1,0:T(8,128)(2,1)}, bf16[2,128,1024]{2,1,0:T(8,128)(2,1)}) custom-call(s32[4,128]{1,0:T(4,128)} %bitcast.16, bf16[4,128]{1,0:T(4,128)(2,1)} %bitcast.19, bf16[2,1344,768]{2,1,0:T(8,128)(2,1)} %get-tuple-element.15.hg_ref, ...), custom_call_target="tpu_custom_call" | custom-call | flops 8455716864 | bytes 33554432 | tf_op jit(solution)/shard_map/weight_grads/pallas_call | solution.py:262
  129.5 24.3 %all-to-all-done.1 = bf16[128,8,1536]{2,1,0:T(8,128)(2,1)S(1)} async-done(((bf16[128,8,1536]{2,1,0:T(8,128)(2,1)}), bf16[128,8,1536]{2,1,0:T(8,128)(2,1)S(1)}, u32[]{:S(2)}, u32[]{:S(2)}) %all-to-all-start.1) | async-done | bytes 3145760 | tf_op jit(solution)/shard_map/all_to_all | solution.py:318
  153.8 0.0 copy-done
  153.8 0.0 copy-done.1
  153.8 0.0 copy-done.2
  153.8 3.7 %combine_back.1 = (bf16[128,1024]{1,0:T(8,128)(2,1)}, f32[4,128]{1,0:T(4,128)}) custom-call(s32[4,128]{1,0:T(4,128)S(1)} %bitcast.17, bf16[4,128]{1,0:T(4,128)(2,1)S(1)} %bitcast.20, bf16[128,1024]{1,0:T(8,128)(2,1)S(1)} %copy-done, bf16[3,128,1024]{2,1,0:T(8,128)(2,1)} %get-tuple-element.19.masks_hbm, bf16[2,128,1024]{2,1,0:T(8,128)(2,1)} %get-tuple-element.20.spread_hbm, ...), custom_call_target="tpu_custom_call" | custom-call | tf_op jit(solution)/shard_map/combine_back/pallas_call | solution.py:305
  (2 shorter events, 0.0 us)
Async XLA Ops:
  0.6 88.6 %slice-start = ((s8[5505024]{0:T(1024)(128)(4,1)}), s8[4194304]{0:T(1024)(128)(4,1)S(1)}, s32[]{:S(2)}) async-start(s8[5505024]{0:T(1024)(128)(4,1)} %bitcast.21), calls=%async_computation.2 | async-start | bytes 8388608
  0.6 88.6 %slice-start.2 = ((s8[5505024]{0:T(1024)(128)(4,1)}), s8[4194304]{0:T(1024)(128)(4,1)S(1)}, s32[]{:S(2)}) async-start(s8[5505024]{0:T(1024)(128)(4,1)} %bitcast.24), calls=%async_computation.4 | async-start | bytes 8388608
  3.0 86.2 %slice-start.1 = ((s8[5505024]{0:T(1024)(128)(4,1)}), s8[1310720]{0:T(1024)(128)(4,1)S(1)}, s32[]{:S(2)}) async-start(s8[5505024]{0:T(1024)(128)(4,1)} %bitcast.21), calls=%async_computation.3 | async-start | bytes 2621440
  3.0 86.2 %slice-start.3 = ((s8[5505024]{0:T(1024)(128)(4,1)}), s8[1310720]{0:T(1024)(128)(4,1)S(1)}, s32[]{:S(2)}) async-start(s8[5505024]{0:T(1024)(128)(4,1)} %bitcast.24), calls=%async_computation.5 | async-start | bytes 2621440
  108.2 45.6 %all-to-all-start.1 = ((bf16[128,8,1536]{2,1,0:T(8,128)(2,1)}), bf16[128,8,1536]{2,1,0:T(8,128)(2,1)S(1)}, u32[]{:S(2)}, u32[]{:S(2)}) async-start(bf16[128,8,1536]{2,1,0:T(8,128)(2,1)} %bitcast.26), calls=%async_computation.1 | async-start | bytes 6291456 | tf_op jit(solution)/shard_map/all_to_all | solution.py:318
  112.7 41.1 %copy-start = (bf16[128,1024]{1,0:T(8,128)(2,1)S(1)}, bf16[128,1024]{1,0:T(8,128)(2,1)}, u32[]{:S(2)}) copy-start(bf16[128,1024]{1,0:T(8,128)(2,1)} %lat_ref.1) | copy-start | bytes 786436
  112.7 41.1 %copy-start.1 = (s32[128,4]{0,1:T(4,128)S(1)}, s32[128,4]{0,1:T(4,128)}, u32[]{:S(2)}) copy-start(s32[128,4]{0,1:T(4,128)} %param.8) | copy-start | bytes 6148
  112.8 41.0 %copy-start.2 = (bf16[128,4]{0,1:T(4,128)(2,1)S(1)}, bf16[128,4]{0,1:T(4,128)(2,1)}, u32[]{:S(2)}) copy-start(bf16[128,4]{0,1:T(4,128)(2,1)} %param.9) | copy-start | bytes 3076

commit v5 on v4

--- a/solution.py
+++ b/solution.py
@@ -151,8 +151,8 @@
     take, take_tail = slot_order(square, 0, False), slot_order(square, 0, True)
 
     def unfold(i, carry):
-        raw = pl.ds(pl.multiple_of(i * GROUP, GROUP), GROUP)
-        at = pl.multiple_of(i * first, second)
+        raw = pl.ds(i * GROUP, GROUP)
+        at = i * first
         whole, head, tail = pl.ds(at, first), pl.ds(at, second), pl.ds(at + second, quarter)
         for to, cols in ((x_s, slice(0, width)), (g_s, slice(width, 2 * width))):
             moved = dot(take, recv_ref[raw, cols]).astype(BF16)
@@ -163,25 +163,18 @@
         g_s[1, tail, :] = moved[quarter:]
         return carry
 
-    lax.fori_loop(0, groups, unfold, 0)
+    for i in range(groups):
+        unfold(i, 0)
     for j in range(exp_local):
         keep(0, j).start()
         keep(1, j).start()
 
-    blocks = 1
-    block = hidden // blocks
     for j in range(exp_local):
-
-        def forward(i, carry):
-            at = pl.ds(pl.multiple_of(i * block, 64), block)
-            pre = dot(up_ref[0, j, at, :], x_s[j], NT)
-            pulled = dot(down_ref[0, j, at, :], g_s[j], NT)
-            act = jnp.maximum(pre, 0.0)
-            sq_s[j, at, :] = (act * act).astype(BF16)
-            hg_s[j, at, :] = (2.0 * act * pulled).astype(BF16)
-            return carry
-
-        lax.fori_loop(0, blocks, forward, 0)
+        pre = dot(up_ref[0, j], x_s[j], NT)
+        pulled = dot(down_ref[0, j], g_s[j], NT)
+        act = jnp.maximum(pre, 0.0)
+        sq_s[j] = (act * act).astype(BF16)
+        hg_s[j] = (2.0 * act * pulled).astype(BF16)
         keep(2, j).start()
         keep(3, j).start()
         y_s[j] = dot(hg_s[j], up_ref[0, j], TN).astype(BF16)
@@ -189,12 +182,12 @@
     put, put_tail = slot_order(square, 1, False), slot_order(square, 1, True)
 
     def copy_out(i):
-        raw = pl.ds(pl.multiple_of(i * GROUP, GROUP), GROUP)
+        raw = pl.ds(i * GROUP, GROUP)
         return pltpu.make_async_copy(back_s.at[raw], back_hbm.at[raw], back_sems.at[i])
 
     def fold(i, carry):
-        raw = pl.ds(pl.multiple_of(i * GROUP, GROUP), GROUP)
-        at = pl.multiple_of(i * first, second)
+        raw = pl.ds(i * GROUP, GROUP)
+        at = i * first
         whole, head, tail = pl.ds(at, first), pl.ds(at, second), pl.ds(at + second, quarter)
         main = jnp.concatenate([y_s[0, whole, :], y_s[1, head, :]], axis=0)
         back_s[raw, :width] = dot(put, main).astype(BF16)
@@ -203,7 +196,8 @@
         copy_out(i).start()
         return carry
 
-    lax.fori_loop(0, groups, fold, 0)
+    for i in range(groups):
+        fold(i, 0)
     for i in range(groups):
         copy_out(i).wait()
     for which in range(4):
@@ -281,20 +275,23 @@
     load_spread = pltpu.make_async_copy(spread_hbm, spread_s, sems.at[1])
     load_masks.start()
     load_spread.start()
+    tail = back_ref[:, width:]
     front_dots = dot(lat_ref[...], back_ref[:, :width], NT)
-    low_dots = dot(lat_ref[:, :half], back_ref[:, width:], NT)
-    high_dots = dot(lat_ref[:, half:], back_ref[:, width:], NT)
+    tail_dots = dot(jnp.concatenate([lat_ref[:, :half], lat_ref[:, half:]], axis=0), tail, NT)
     load_masks.wait()
-    main, low, high = (masks_s[i] for i in range(3))
-    tail = back_ref[:, width:]
-    lat_out[:, :half] = (dot(main, back_ref[:, :half]) + dot(low, tail)).astype(BF16)
-    lat_out[:, half:] = (dot(main, back_ref[:, half:width]) + dot(high, tail)).astype(BF16)
+    main = masks_s[0]
+    rest = jnp.concatenate([masks_s[1], masks_s[2]], axis=0)
+    front_rows, tail_rows = dot(main, back_ref[:, :width]), dot(rest, tail)
+    lat_out[:, :half] = (front_rows[:, :half] + tail_rows[:tokens]).astype(BF16)
+    lat_out[:, half:] = (front_rows[:, half:] + tail_rows[tokens:]).astype(BF16)
     load_spread.wait()
-    gained = jnp.zeros((experts, tokens), F32)
-    for i, dots in enumerate((main.astype(F32) * front_dots, low.astype(F32) * low_dots + high.astype(F32) * high_dots)):
+    tail_dots = rest.astype(F32) * tail_dots
+    gained = jnp.zeros((experts, 2 * tokens), F32)
+    for i, dots in enumerate((main.astype(F32) * front_dots, tail_dots[:tokens] + tail_dots[tokens:])):
         upper = dots.astype(BF16)
         lower = (dots - upper.astype(F32)).astype(BF16)
-        gained = gained + dot(spread_s[i], upper, NT) + dot(spread_s[i], lower, NT)
+        gained = gained + dot(spread_s[i], jnp.concatenate([upper, lower], axis=0), NT)
+    gained = gained[:, :tokens] + gained[:, tokens:]
     e_at = iota((experts, tokens), 0)
     for k in range(picks):
         dots = jnp.sum(jnp.where(ids_ref[k : k + 1, :] == e_at, gained, 0.0), axis=0, keepdims=True)

time: 158 us -> 156 us (0.987)
  Pallas kernels: 41.7 us -> 39.9 us
where the time goes in v5:
time: 156 us
  blocking collectives  86.2 us (55%)
  Pallas kernels  39.9 us (26%)
  waiting for transfers between devices  24.3 us (16%)
  starting transfers between devices  4.53 us (3%)
    all_to_all x1, blocking collectives, exchange(): lax.all_to_all(rows.reshape(owners, SUB, shape[1]), AXES, split_axis=0, c...  86.2 us
    all_to_all x1, waiting for transfers between devices, exchange(): lax.all_to_all(rows.reshape(owners, SUB, shape[1]), AXES, split_axis=0, c...  24.3 us
    pallas_call x1, Pallas kernels, expert_rows(): pl.pallas_call(rows_kernel, in_specs=[IN_VMEM] * 3, out_specs=[IN_HBM] *...  17.5 us
    pallas_call x1, Pallas kernels, weight_grads(): pl.pallas_call(functools.partial(weights_kernel, experts), grid=(exp_loca...  16.7 us
    all_to_all x1, starting transfers between devices, exchange(): lax.all_to_all(rows.reshape(owners, SUB, shape[1]), AXES, split_axis=0, c...  4.53 us
    pallas_call x1, Pallas kernels, combine_back(): pl.pallas_call(combine_kernel, in_specs=[IN_VMEM] * 3 + [IN_HBM] * 2 + [I...  3.3 us
  transfers between devices with their start and end apart: 1, of which 1 were waited for; matrix products, arithmetic and copies ran while one was open for 0% of the time, Pallas kernels for 11%

profile of v5, /device:TPU:1, one launch (start us, length us, event | category | flops | bytes accessed | tf_op | source)
XLA Modules:
  0.0 155.9 jit_solution(18257745056354278750)
XLA Ops:
  0.6 0.0 slice-start
  0.6 0.0 slice-start.2
  0.7 2.4 %pack.1 = bf16[1024,3072]{1,0:T(8,128)(2,1)S(1)} custom-call(s32[4,128]{1,0:T(4,128)} %bitcast.15, bf16[4,128]{1,0:T(4,128)(2,1)} %bitcast.18, bf16[128,1024]{1,0:T(8,128)(2,1)} %lat_ref.1, bf16[128,1024]{1,0:T(8,128)(2,1)} %grad_hbm.1), custom_call_target="tpu_custom_call" | custom-call | flops 1073741824 | bytes 6291456 | tf_op jit(solution)/shard_map/pack/pallas_call | solution.py:107
  3.0 0.0 slice-start.1
  3.0 0.0 slice-start.3
  3.1 86.2 %all_to_all.10 = bf16[128,8,3072]{2,1,0:T(8,128)(2,1)S(1)} all-to-all(bf16[128,8,3072]{2,1,0:T(8,128)(2,1)S(1)} %bitcast.12), channel_id=1, replica_groups=mesh['node'=8,'local'=16] {'node','local'}, dimensions={0} | all-to-all | bytes 12582912 | tf_op jit(solution)/shard_map/all_to_all | solution.py:315
  89.2 0.0 slice-done
  89.2 0.0 slice-done.2
  89.2 0.0 slice-done.1
  89.2 0.0 slice-done.3
  89.3 17.5 %expert_rows.1 = (bf16[2,768,1024]{2,1,0:T(8,128)(2,1)}, bf16[2,768,1024]{2,1,0:T(8,128)(2,1)}, bf16[2,1344,768]{2,1,0:T(8,128)(2,1)}, bf16[2,1344,768]{2,1,0:T(8,128)(2,1)}, bf16[1024,1536]{1,0:T(8,128)(2,1)}) custom-call(bf16[1024,3072]{1,0:T(8,128)(2,1)S(1)} %bitcast.14, bf16[1,2,1344,1024]{3,2,1,0:T(8,128)(2,1)S(1)} %bitcast.23, ...), custom_call_target="tpu_custom_call" | custom-call | flops 12683575296 | bytes 33554432 | tf_op jit(solution)/shard_map/expert_rows/pallas_call | solution.py:214
  106.8 4.5 %all-to-all-start.1 = ((bf16[128,8,1536]{2,1,0:T(8,128)(2,1)}), bf16[128,8,1536]{2,1,0:T(8,128)(2,1)S(1)}, u32[]{:S(2)}, u32[]{:S(2)}) async-start(bf16[128,8,1536]{2,1,0:T(8,128)(2,1)} %bitcast.26), calls=%async_computation.1 | async-start | bytes 6291456 | tf_op jit(solution)/shard_map/all_to_all | solution.py:315
  111.3 0.0 copy-start
  111.4 0.0 copy-start.1
  111.4 0.0 copy-start.2
  111.4 16.7 %weight_grads.1 = (bf16[2,1344,1024]{2,1,0:T(8,128)(2,1)}, bf16[2,1344,1024]{2,1,0:T(8,128)(2,1)}, bf16[3,128,1024]{2,1,0:T(8,128)(2,1)}, bf16[2,128,1024]{2,1,0:T(8,128)(2,1)}) custom-call(s32[4,128]{1,0:T(4,128)} %bitcast.16, bf16[4,128]{1,0:T(4,128)(2,1)} %bitcast.19, bf16[2,1344,768]{2,1,0:T(8,128)(2,1)} %get-tuple-element.15.hg_ref, ...), custom_call_target="tpu_custom_call" | custom-call | flops 8455716864 | bytes 33554432 | tf_op jit(solution)/shard_map/weight_grads/pallas_call | solution.py:256
  128.1 24.3 %all-to-all-done.1 = bf16[128,8,1536]{2,1,0:T(8,128)(2,1)S(1)} async-done(((bf16[128,8,1536]{2,1,0:T(8,128)(2,1)}), bf16[128,8,1536]{2,1,0:T(8,128)(2,1)S(1)}, u32[]{:S(2)}, u32[]{:S(2)}) %all-to-all-start.1) | async-done | bytes 3145760 | tf_op jit(solution)/shard_map/all_to_all | solution.py:315
  152.4 0.0 copy-done
  152.4 0.0 copy-done.1
  152.4 0.0 copy-done.2
  152.4 3.3 %combine_back.1 = (bf16[128,1024]{1,0:T(8,128)(2,1)}, f32[4,128]{1,0:T(4,128)}) custom-call(s32[4,128]{1,0:T(4,128)S(1)} %bitcast.17, bf16[4,128]{1,0:T(4,128)(2,1)S(1)} %bitcast.20, bf16[128,1024]{1,0:T(8,128)(2,1)S(1)} %copy-done, bf16[3,128,1024]{2,1,0:T(8,128)(2,1)} %get-tuple-element.19.masks_hbm, bf16[2,128,1024]{2,1,0:T(8,128)(2,1)} %get-tuple-element.20.spread_hbm, ...), custom_call_target="tpu_custom_call" | custom-call | tf_op jit(solution)/shard_map/combine_back/pallas_call | solution.py:302
  (2 shorter events, 0.0 us)
Async XLA Ops:
  0.6 88.6 %slice-start = ((s8[5505024]{0:T(1024)(128)(4,1)}), s8[4194304]{0:T(1024)(128)(4,1)S(1)}, s32[]{:S(2)}) async-start(s8[5505024]{0:T(1024)(128)(4,1)} %bitcast.21), calls=%async_computation.2 | async-start | bytes 8388608
  0.6 88.6 %slice-start.2 = ((s8[5505024]{0:T(1024)(128)(4,1)}), s8[4194304]{0:T(1024)(128)(4,1)S(1)}, s32[]{:S(2)}) async-start(s8[5505024]{0:T(1024)(128)(4,1)} %bitcast.24), calls=%async_computation.4 | async-start | bytes 8388608
  3.0 86.2 %slice-start.1 = ((s8[5505024]{0:T(1024)(128)(4,1)}), s8[1310720]{0:T(1024)(128)(4,1)S(1)}, s32[]{:S(2)}) async-start(s8[5505024]{0:T(1024)(128)(4,1)} %bitcast.21), calls=%async_computation.3 | async-start | bytes 2621440
  3.0 86.2 %slice-start.3 = ((s8[5505024]{0:T(1024)(128)(4,1)}), s8[1310720]{0:T(1024)(128)(4,1)S(1)}, s32[]{:S(2)}) async-start(s8[5505024]{0:T(1024)(128)(4,1)} %bitcast.24), calls=%async_computation.5 | async-start | bytes 2621440
  106.8 45.6 %all-to-all-start.1 = ((bf16[128,8,1536]{2,1,0:T(8,128)(2,1)}), bf16[128,8,1536]{2,1,0:T(8,128)(2,1)S(1)}, u32[]{:S(2)}, u32[]{:S(2)}) async-start(bf16[128,8,1536]{2,1,0:T(8,128)(2,1)} %bitcast.26), calls=%async_computation.1 | async-start | bytes 6291456 | tf_op jit(solution)/shard_map/all_to_all | solution.py:315
  111.3 41.1 %copy-start = (bf16[128,1024]{1,0:T(8,128)(2,1)S(1)}, bf16[128,1024]{1,0:T(8,128)(2,1)}, u32[]{:S(2)}) copy-start(bf16[128,1024]{1,0:T(8,128)(2,1)} %lat_ref.1) | copy-start | bytes 786436
  111.4 41.1 %copy-start.1 = (s32[128,4]{0,1:T(4,128)S(1)}, s32[128,4]{0,1:T(4,128)}, u32[]{:S(2)}) copy-start(s32[128,4]{0,1:T(4,128)} %param.8) | copy-start | bytes 6148
  111.4 41.0 %copy-start.2 = (bf16[128,4]{0,1:T(4,128)(2,1)S(1)}, bf16[128,4]{0,1:T(4,128)(2,1)}, u32[]{:S(2)}) copy-start(bf16[128,4]{0,1:T(4,128)(2,1)} %param.9) | copy-start | bytes 3076

commit v6 on v5

--- a/solution.py
+++ b/solution.py
@@ -169,12 +169,14 @@
         keep(0, j).start()
         keep(1, j).start()
 
+    acts, pulls = [], []
     for j in range(exp_local):
-        pre = dot(up_ref[0, j], x_s[j], NT)
-        pulled = dot(down_ref[0, j], g_s[j], NT)
-        act = jnp.maximum(pre, 0.0)
+        acts.append(dot(up_ref[0, j], x_s[j], NT))
+        pulls.append(dot(down_ref[0, j], g_s[j], NT))
+    for j in range(exp_local):
+        act = jnp.maximum(acts[j], 0.0)
         sq_s[j] = (act * act).astype(BF16)
-        hg_s[j] = (2.0 * act * pulled).astype(BF16)
+        hg_s[j] = (2.0 * act * pulls[j]).astype(BF16)
         keep(2, j).start()
         keep(3, j).start()
         y_s[j] = dot(hg_s[j], up_ref[0, j], TN).astype(BF16)

time: 156 us -> 156 us (level)
  no operation moved by 1% of the time
where the time goes in v6:
time: 156 us
  blocking collectives  86.2 us (55%)
  Pallas kernels  39.9 us (26%)
  waiting for transfers between devices  24.3 us (16%)
  starting transfers between devices  4.53 us (3%)
    all_to_all x1, blocking collectives, exchange(): lax.all_to_all(rows.reshape(owners, SUB, shape[1]), AXES, split_axis=0, c...  86.2 us
    all_to_all x1, waiting for transfers between devices, exchange(): lax.all_to_all(rows.reshape(owners, SUB, shape[1]), AXES, split_axis=0, c...  24.3 us
    pallas_call x1, Pallas kernels, expert_rows(): pl.pallas_call(rows_kernel, in_specs=[IN_VMEM] * 3, out_specs=[IN_HBM] *...  17.5 us
    pallas_call x1, Pallas kernels, weight_grads(): pl.pallas_call(functools.partial(weights_kernel, experts), grid=(exp_loca...  16.7 us
    all_to_all x1, starting transfers between devices, exchange(): lax.all_to_all(rows.reshape(owners, SUB, shape[1]), AXES, split_axis=0, c...  4.53 us
    pallas_call x1, Pallas kernels, combine_back(): pl.pallas_call(combine_kernel, in_specs=[IN_VMEM] * 3 + [IN_HBM] * 2 + [I...  3.3 us
  transfers between devices with their start and end apart: 1, of which 1 were waited for; matrix products, arithmetic and copies ran while one was open for 0% of the time, Pallas kernels for 11%

profile of v6, /device:TPU:1, one launch (start us, length us, event | category | flops | bytes accessed | tf_op | source)
XLA Modules:
  0.0 155.9 jit_solution(2794170540873986636)
XLA Ops:
  0.6 0.0 slice-start
  0.6 0.0 slice-start.2
  0.7 2.4 %pack.1 = bf16[1024,3072]{1,0:T(8,128)(2,1)S(1)} custom-call(s32[4,128]{1,0:T(4,128)} %bitcast.15, bf16[4,128]{1,0:T(4,128)(2,1)} %bitcast.18, bf16[128,1024]{1,0:T(8,128)(2,1)} %lat_ref.1, bf16[128,1024]{1,0:T(8,128)(2,1)} %grad_hbm.1), custom_call_target="tpu_custom_call" | custom-call | flops 1073741824 | bytes 6291456 | tf_op jit(solution)/shard_map/pack/pallas_call | solution.py:107
  3.0 0.0 slice-start.1
  3.0 0.0 slice-start.3
  3.1 86.2 %all_to_all.10 = bf16[128,8,3072]{2,1,0:T(8,128)(2,1)S(1)} all-to-all(bf16[128,8,3072]{2,1,0:T(8,128)(2,1)S(1)} %bitcast.12), channel_id=1, replica_groups=mesh['node'=8,'local'=16] {'node','local'}, dimensions={0} | all-to-all | bytes 12582912 | tf_op jit(solution)/shard_map/all_to_all | solution.py:317
  89.2 0.0 slice-done
  89.2 0.0 slice-done.2
  89.2 0.0 slice-done.1
  89.2 0.0 slice-done.3
  89.3 17.5 %expert_rows.1 = (bf16[2,768,1024]{2,1,0:T(8,128)(2,1)}, bf16[2,768,1024]{2,1,0:T(8,128)(2,1)}, bf16[2,1344,768]{2,1,0:T(8,128)(2,1)}, bf16[2,1344,768]{2,1,0:T(8,128)(2,1)}, bf16[1024,1536]{1,0:T(8,128)(2,1)}) custom-call(bf16[1024,3072]{1,0:T(8,128)(2,1)S(1)} %bitcast.14, bf16[1,2,1344,1024]{3,2,1,0:T(8,128)(2,1)S(1)} %bitcast.23, ...), custom_call_target="tpu_custom_call" | custom-call | flops 12683575296 | bytes 33554432 | tf_op jit(solution)/shard_map/expert_rows/pallas_call | solution.py:216
  106.8 4.5 %all-to-all-start.1 = ((bf16[128,8,1536]{2,1,0:T(8,128)(2,1)}), bf16[128,8,1536]{2,1,0:T(8,128)(2,1)S(1)}, u32[]{:S(2)}, u32[]{:S(2)}) async-start(bf16[128,8,1536]{2,1,0:T(8,128)(2,1)} %bitcast.26), calls=%async_computation.1 | async-start | bytes 6291456 | tf_op jit(solution)/shard_map/all_to_all | solution.py:317
  111.4 0.0 copy-start
  111.4 0.0 copy-start.1
  111.4 0.0 copy-start.2
  111.4 16.7 %weight_grads.1 = (bf16[2,1344,1024]{2,1,0:T(8,128)(2,1)}, bf16[2,1344,1024]{2,1,0:T(8,128)(2,1)}, bf16[3,128,1024]{2,1,0:T(8,128)(2,1)}, bf16[2,128,1024]{2,1,0:T(8,128)(2,1)}) custom-call(s32[4,128]{1,0:T(4,128)} %bitcast.16, bf16[4,128]{1,0:T(4,128)(2,1)} %bitcast.19, bf16[2,1344,768]{2,1,0:T(8,128)(2,1)} %get-tuple-element.15.hg_ref, ...), custom_call_target="tpu_custom_call" | custom-call | flops 8455716864 | bytes 33554432 | tf_op jit(solution)/shard_map/weight_grads/pallas_call | solution.py:258
  128.1 24.3 %all-to-all-done.1 = bf16[128,8,1536]{2,1,0:T(8,128)(2,1)S(1)} async-done(((bf16[128,8,1536]{2,1,0:T(8,128)(2,1)}), bf16[128,8,1536]{2,1,0:T(8,128)(2,1)S(1)}, u32[]{:S(2)}, u32[]{:S(2)}) %all-to-all-start.1) | async-done | bytes 3145760 | tf_op jit(solution)/shard_map/all_to_all | solution.py:317
  152.4 0.0 copy-done
  152.4 0.0 copy-done.1
  152.4 0.0 copy-done.2
  152.4 3.3 %combine_back.1 = (bf16[128,1024]{1,0:T(8,128)(2,1)}, f32[4,128]{1,0:T(4,128)}) custom-call(s32[4,128]{1,0:T(4,128)S(1)} %bitcast.17, bf16[4,128]{1,0:T(4,128)(2,1)S(1)} %bitcast.20, bf16[128,1024]{1,0:T(8,128)(2,1)S(1)} %copy-done, bf16[3,128,1024]{2,1,0:T(8,128)(2,1)} %get-tuple-element.19.masks_hbm, bf16[2,128,1024]{2,1,0:T(8,128)(2,1)} %get-tuple-element.20.spread_hbm, ...), custom_call_target="tpu_custom_call" | custom-call | tf_op jit(solution)/shard_map/combine_back/pallas_call | solution.py:304
  (2 shorter events, 0.0 us)
Async XLA Ops:
  0.6 88.6 %slice-start = ((s8[5505024]{0:T(1024)(128)(4,1)}), s8[4194304]{0:T(1024)(128)(4,1)S(1)}, s32[]{:S(2)}) async-start(s8[5505024]{0:T(1024)(128)(4,1)} %bitcast.21), calls=%async_computation.2 | async-start | bytes 8388608
  0.6 88.6 %slice-start.2 = ((s8[5505024]{0:T(1024)(128)(4,1)}), s8[4194304]{0:T(1024)(128)(4,1)S(1)}, s32[]{:S(2)}) async-start(s8[5505024]{0:T(1024)(128)(4,1)} %bitcast.24), calls=%async_computation.4 | async-start | bytes 8388608
  3.0 86.2 %slice-start.1 = ((s8[5505024]{0:T(1024)(128)(4,1)}), s8[1310720]{0:T(1024)(128)(4,1)S(1)}, s32[]{:S(2)}) async-start(s8[5505024]{0:T(1024)(128)(4,1)} %bitcast.21), calls=%async_computation.3 | async-start | bytes 2621440
  3.0 86.2 %slice-start.3 = ((s8[5505024]{0:T(1024)(128)(4,1)}), s8[1310720]{0:T(1024)(128)(4,1)S(1)}, s32[]{:S(2)}) async-start(s8[5505024]{0:T(1024)(128)(4,1)} %bitcast.24), calls=%async_computation.5 | async-start | bytes 2621440
  106.8 45.6 %all-to-all-start.1 = ((bf16[128,8,1536]{2,1,0:T(8,128)(2,1)}), bf16[128,8,1536]{2,1,0:T(8,128)(2,1)S(1)}, u32[]{:S(2)}, u32[]{:S(2)}) async-start(bf16[128,8,1536]{2,1,0:T(8,128)(2,1)} %bitcast.26), calls=%async_computation.1 | async-start | bytes 6291456 | tf_op jit(solution)/shard_map/all_to_all | solution.py:317
  111.4 41.1 %copy-start = (bf16[128,1024]{1,0:T(8,128)(2,1)S(1)}, bf16[128,1024]{1,0:T(8,128)(2,1)}, u32[]{:S(2)}) copy-start(bf16[128,1024]{1,0:T(8,128)(2,1)} %lat_ref.1) | copy-start | bytes 786436
  111.4 41.0 %copy-start.1 = (s32[128,4]{0,1:T(4,128)S(1)}, s32[128,4]{0,1:T(4,128)}, u32[]{:S(2)}) copy-start(s32[128,4]{0,1:T(4,128)} %param.8) | copy-start | bytes 6148
  111.4 41.0 %copy-start.2 = (bf16[128,4]{0,1:T(4,128)(2,1)S(1)}, bf16[128,4]{0,1:T(4,128)(2,1)}, u32[]{:S(2)}) copy-start(bf16[128,4]{0,1:T(4,128)(2,1)} %param.9) | copy-start | bytes 3076
